TPU v7x, 32 devices: a whole 2x2x4 slice. The times are simulated.
32 devices in a mesh: gx: 4 (over y, core), gy: 8 (over z, x).
Axes of the slice: x: 2, y: 2, z: 4, core: 2. Of those that a mesh axis runs over, the one named last changes fastest.
Arguments:
- multipoles: bfloat16 [136, 2048], P(None, ('gx', 'gy')), may hold values from -6 to 6
- parent_ops: bfloat16 [4, 36992], replicated, may hold values from -0.1875 to 0.1875
- translators: bfloat16 [158, 36992], replicated, may hold values from -0.0390625 to 0.0390625
- fine_exports: int32 [32, 8, 32], P(('gx', 'gy')), may hold values from 0 to 63, as said below
- fine_sides: int32 [32, 2, 16], P(('gx', 'gy')), may hold values from 0 to 63, as said below
- fine_lists: int32 [189, 2048], P(None, ('gx', 'gy')), may hold values from 0 to 351
- fine_flags: int32 [189, 2048], P(None, ('gx', 'gy')), may hold values 0 or 1
- coarse_exports: int32 [32, 8, 4], P(('gx', 'gy')), may hold values from 0 to 7, as said below
- coarse_sides: int32 [32, 2, 2], P(('gx', 'gy')), may hold values from 0 to 7, as said below
- coarse_lists: int32 [189, 256], P(None, ('gx', 'gy')), may hold values from 0 to 43
- coarse_flags: int32 [189, 256], P(None, ('gx', 'gy')), may hold values 0 or 1
Outputs:
- fine_locals: float32 [136, 2048], P(None, ('gx', 'gy'))
- coarse_locals: float32 [136, 256], P(None, ('gx', 'gy'))
Inputs may be any that keep to these rules, and one draw needn't show every extreme that they name: `fine_sides`: entries of the exports and sides are cells of the sending device, distinct within each row; the first row of sides goes to the next gx row, the second to the previous one. `fine_exports`: entries are cells of the sending device, distinct within each row. `coarse_exports`: entries are coarse cells of the sending device, distinct within each row. `coarse_sides`: entries are coarse cells of the sending device, distinct within each row. `fine_lists`: A list entry names a place in the owning device's fine source buffer. `coarse_lists`: A list entry names a place in the owning device's coarse source buffer.
All inputs are finite; a program needn't handle non-finite values. No bound on the sum of `fine_flags` or of `coarse_flags` on one device may be relied on, other than what follows from the above.
Results may differ from a plain program's by a relative error of at most 0.0029.
Values may be sent and summed in bfloat16 or wider, within the bound.
A program may use at most 128 MiB of HBM per device.

v0:
```python
import jax
import jax.numpy as jnp
import numpy as np
from jax import lax
from jax.sharding import PartitionSpec as P


def passed_along(block, axis, distance):
    devices = range(lax.axis_size(axis))
    route = [(i - distance, i) for i in devices if i - distance in devices]
    return lax.ppermute(block, axis, route)


def direction_table():
    far_offsets = {}
    for shift_x in range(-3, 4):
        for shift_y in range(-3, 4):
            for shift_z in range(-3, 4):
                if max(abs(shift_x), abs(shift_y), abs(shift_z)) > 1:
                    far_offsets[shift_x, shift_y, shift_z] = len(far_offsets)
    result = np.zeros((8, 189), np.int32)
    for octant in range(8):
        own_x, own_y, own_z = (octant % 2, octant // 2 % 2, octant // 4)
        column = 0
        for parent_x in (-1, 0, 1):
            for parent_y in (-1, 0, 1):
                for parent_z in (-1, 0, 1):
                    for child in range(8):
                        step_x = 2 * parent_x + child % 2 - own_x
                        step_y = 2 * parent_y + child // 2 % 2 - own_y
                        step_z = 2 * parent_z + child // 4 - own_z
                        if max(abs(step_x), abs(step_y), abs(step_z)) > 1:
                            result[octant, column] = far_offsets[step_x, step_y, step_z]
                            column = column + 1
    return result


def entry_of_offset(dir_table, offset_count):
    entries = dir_table.shape[1]
    inverse = np.full((offset_count, 8), entries, np.int32)
    for octant in range(8):
        for entry in range(entries):
            inverse[dir_table[octant, entry], octant] = entry
    return inverse


def fetch(levels):
    upward = jnp.concatenate(
        [jnp.take(level[0], level[2][0, 0], axis=1) for level in levels], axis=1
    )
    downward = jnp.concatenate(
        [jnp.take(level[0], level[2][0, 1], axis=1) for level in levels], axis=1
    )
    below = passed_along(upward, "gx", 1)
    above = passed_along(downward, "gx", -1)
    row_pieces = []
    row_parts = jnp.concatenate(
        [jnp.take(level[0], level[1][0], axis=1) for level in levels], axis=2
    )
    received = lax.all_to_all(row_parts, "gy", split_axis=1, concat_axis=1, tiled=True)
    row_start = 0
    for level in levels:
        cap_row = level[1].shape[2]
        row_pieces.append(received.reshape(level[0].shape[0], -1))
        row_start = row_start + cap_row
    buffers = []
    side_start = 0
    for level, from_row in zip(levels, row_pieces):
        side_cells = level[2].shape[2]
        buffers.append(jnp.concatenate([level[0], from_row, below, above], axis=1))
        side_start = side_start + side_cells
    return buffers


def translate(buffer, lists, flags, offset_ops, inverse):
    cell_count = lists.shape[1]
    pad_row = jnp.zeros((1, cell_count), jnp.int32)
    lists_ext = jnp.concatenate([lists, pad_row], axis=0)
    flags_ext = jnp.concatenate([flags, pad_row], axis=0)
    rows_table = jnp.asarray(np.tile(inverse, (1, cell_count // 8)))
    picks = jnp.take_along_axis(lists_ext, rows_table, axis=0)
    live = jnp.take_along_axis(flags_ext, rows_table, axis=0)
    gathered = jnp.take(buffer, picks, axis=1)
    gathered = jnp.where(live[None] > 0, gathered, jnp.zeros_like(gathered))
    return jnp.einsum("tkl,ltc->kc", offset_ops, gathered, preferred_element_type=jnp.float32)


def shards(
    multipoles,
    parent_ops,
    translators,
    fine_exports,
    fine_sides,
    fine_lists,
    fine_flags,
    coarse_exports,
    coarse_sides,
    coarse_lists,
    coarse_flags,
):
    coeffs = multipoles.shape[0]
    octant_ops = parent_ops.reshape(8, coeffs, coeffs)
    offset_ops = translators.reshape(-1, coeffs, coeffs)
    children = multipoles.reshape(coeffs, -1, 8)
    coarse = jnp.einsum(
        "okl,lqo->kq", octant_ops, children, preferred_element_type=jnp.float32
    ).astype(jnp.bfloat16)
    inverse = entry_of_offset(direction_table(), offset_ops.shape[0])
    fine_buffer = fetch([(multipoles, fine_exports, fine_sides)])[0]
    fine_locals = translate(fine_buffer, fine_lists, fine_flags, offset_ops, inverse)
    coarse_buffer = fetch([(coarse, coarse_exports, coarse_sides)])[0]
    coarse_locals = translate(coarse_buffer, coarse_lists, coarse_flags, offset_ops, inverse)
    return (fine_locals, coarse_locals)


def solution(mesh):
    return jax.shard_map(
        shards,
        mesh=mesh,
        in_specs=(
            P(None, ("gx", "gy")),
            P(),
            P(),
            P(("gx", "gy"), None, None),
            P(("gx", "gy"), None, None),
            P(None, ("gx", "gy")),
            P(None, ("gx", "gy")),
            P(("gx", "gy"), None, None),
            P(("gx", "gy"), None, None),
            P(None, ("gx", "gy")),
            P(None, ("gx", "gy")),
        ),
        out_specs=(P(None, ("gx", "gy")), P(None, ("gx", "gy"))),
        check_vma=False,
    )
```

profile of v0, /device:TPU:0, one launch (start us, length us, event | category | flops | bytes accessed | tf_op | source)
XLA Modules:
  0.0 578.9 jit_solution(5363748515285320633)
XLA Ops:
  0.6 0.8 compare_and_fusion.6
  1.4 1.3 gather_fusion.7
  2.8 0.7 select_bitcast_fusion.2
  3.4 1.3 collective-permute-start.1
  4.7 1.3 gather_fusion.6
  6.1 0.7 select_bitcast_fusion.3
  6.7 3.6 collective-permute-start
  10.4 2.4 reshape.129
  12.8 0.8 compare_and_fusion.4
  13.5 1.0 fusion.11
  14.5 0.6 gather_fusion.11
  15.1 0.6 fusion.21
  15.7 1.3 collective-permute-start.3
  17.0 0.6 gather_fusion.10
  17.6 0.6 fusion.20
  18.2 5.0 collective-permute-start.2
  23.2 0.7 compare_select_fusion.4
  23.9 0.7 compare_and_fusion.7
  24.8 0.6 gather_fusion.2
  25.5 0.7 select_bitcast_fusion.1
  26.2 5.8 %all-to-all-start.1 = ((bf16[136,8,4]{0,2,1:T(4,128)(2,1)}), bf16[136,8,4]{0,2,1:T(4,128)(2,1)}, u32[]{:S(2)}, u32[]{:S(2)}) async-start(bf16[136,8,4]{0,2,1:T(4,128)(2,1)} %select_bitcast_fusion.1), calls=%async_computation.1 | async-start | bytes 32768 | tf_op jit(solution)/shard_map/all_to_all | solution.py:60
  32.0 0.7 compare_select_fusion.2
  32.7 1.2 compare_and_fusion.2
  33.9 0.8 concatenate.19
  34.8 152.0 %gather_fusion.5 = s32[20224]{0:T(1024)S(1)} fusion(s32[190,64]{0,1:T(8,128)S(1)} %concatenate.19, s32[20224]{0:T(1024)S(1)} %copy-done), kind=kCustom, calls=%fused_computation.4.clone | custom fusion | bytes 323584 | tf_op jit(solution)/shard_map/jit(take_along_axis)/gather | solution.py:81
  187.0 0.7 compare_and_fusion.1
  187.7 16.1 %gather_fusion.9 = s32[2528]{0:T(1024)S(1)} fusion(s32[190,8]{0,1:T(8,128)S(1)} %concatenate.22, s32[2528]{0:T(1024)S(1)} %copy-done.3), kind=kCustom, calls=%fused_computation.6.clone | custom fusion | bytes 40448 | tf_op jit(solution)/shard_map/jit(take_along_axis)/gather | solution.py:81
  204.1 1.2 gather_fusion
  205.3 0.7 pad_clamp_fusion
  206.0 152.0 %gather_fusion.4 = s32[20224]{0:T(1024)S(1)} fusion(s32[190,64]{0,1:T(8,128)S(1)} %concatenate.18, s32[20224]{0:T(1024)S(1)} %copy-done), kind=kCustom, calls=%fused_computation.clone | custom fusion | bytes 323584 | tf_op jit(solution)/shard_map/jit(take_along_axis)/gather | solution.py:82
  358.2 0.1 reshape.216
  358.3 16.1 %gather_fusion.8 = s32[2528]{0:T(1024)S(1)} fusion(s32[190,8]{0,1:T(8,128)S(1)} %concatenate.21, s32[2528]{0:T(1024)S(1)} %copy-done.3), kind=kCustom, calls=%fused_computation.2.clone | custom fusion | bytes 40448 | tf_op jit(solution)/shard_map/jit(take_along_axis)/gather | solution.py:82
  374.4 0.1 reshape.244
  374.6 0.8 select_bitcast_fusion
  375.4 62.3 %reshape.128 = bf16[316,136,136]{2,1,0:T(8,128)(2,1)} reshape(bf16[158,36992]{1,0:T(8,128)(2,1)} %param.23) | data formatting | bytes 23378944 | tf_op jit(solution)/shard_map/reshape | solution.py:103
  437.7 33.0 %copy.25 = bf16[316,136,136]{0,1,2:T(8,128)(2,1)} copy(bf16[316,136,136]{2,1,0:T(8,128)(2,1)} %reshape.128) | data formatting | bytes 23378944 | tf_op jit(solution)/shard_map/reshape | solution.py:103
  470.7 0.1 copy.22
  470.8 0.1 copy.23
  471.2 6.0 %all-to-all-start = ((bf16[136,8,32]{0,2,1:T(8,128)(2,1)}), bf16[136,8,32]{0,2,1:T(8,128)(2,1)S(1)}, u32[]{:S(2)}, u32[]{:S(2)}) async-start(bf16[136,8,32]{0,2,1:T(8,128)(2,1)} %select_bitcast_fusion), calls=%async_computation | async-start | bytes 262144 | tf_op jit(solution)/shard_map/all_to_all | solution.py:60
  477.2 0.7 reshape.131
  478.0 0.7 pad_maximum_fusion.1
  478.7 7.8 %gather_fusion.3 = bf16[2528,136]{1,0:T(8,128)(2,1)S(1)} fusion(bf16[136,44]{0,1:T(8,128)(2,1)S(1)} %pad_maximum_fusion.1, s32[3072]{0:T(1024)S(1)} %pad_clamp_fusion.1), kind=kCustom, calls=%fused_computation.11 | custom fusion | bytes 1385344 | tf_op jit(solution)/shard_map/jit(_take)/gather | solution.py:83
  486.5 1.6 copy.31
  488.2 7.6 %convolution_bitcast_fusion = f32[136,8]{0,1:T(8,128)} fusion(bf16[316,136,136]{0,1,2:T(8,128)(2,1)} %copy.25, bf16[316,8,136]{0,1,2:T(8,128)(2,1)S(1)} %copy.31, pred[316,8]{0,1:T(8,128)(4,1)S(1)} %copy.26, pred[316,8]{0,1:T(8,128)(4,1)S(1)} %copy.27), kind=kOutput, calls=%fused_computation.21 | convolution fusion | flops 94203392 | bytes 12386496 | tf_op jit(solution)/shard_map/tkl,ltc->kc/dot_general | solution.py:85
  495.8 0.7 pad_maximum_fusion
  496.5 56.2 %gather_fusion.1 = bf16[20224,136]{1,0:T(8,128)(2,1)} fusion(bf16[136,352]{0,1:T(8,128)(2,1)S(1)} %pad_maximum_fusion, s32[20480]{0:T(1024)S(1)} %copy-done.6), kind=kCustom, calls=%fused_computation.9 | custom fusion | bytes 11082752 | tf_op jit(solution)/shard_map/jit(_take)/gather | solution.py:83
  552.7 16.1 %copy.24 = bf16[316,64,136]{0,1,2:T(8,128)(2,1)} copy(bf16[316,64,136]{2,1,0:T(8,128)(2,1)} %bitcast.72) | data formatting | bytes 11001856 | tf_op jit(solution)/shard_map/jit(_take)/gather | solution.py:83
  568.8 10.1 %fusion.8 = f32[136,64]{0,1:T(8,128)} fusion(bf16[316,136,136]{0,1,2:T(8,128)(2,1)} %copy.25, bf16[316,64,136]{0,1,2:T(8,128)(2,1)} %copy.24, pred[316,64]{0,1:T(8,128)(4,1)S(1)} %copy.22, pred[316,64]{0,1:T(8,128)(4,1)S(1)} %copy.23), kind=kOutput, calls=%fused_computation.20 | convolution fusion | flops 753627136 | bytes 17265664 | tf_op jit(solution)/shard_map/tkl,ltc->kc/dot_general | solution.py:85
  (56 shorter events, 1.2 us)
Async XLA Ops:
  0.6 34.2 %copy-start = (s32[20224]{0:T(1024)S(1)}, s32[20224]{0:T(1024)}, u32[]{:S(2)}) copy-start(s32[20224]{0:T(1024)} %constant.245) | copy-start | bytes 242692
  3.4 492.3 %collective-permute-start.1 = (bf16[136,16]{0,1:T(8,128)(2,1)}, bf16[136,16]{0,1:T(8,128)(2,1)}, u32[]{:S(2)}, u32[]{:S(2)}) collective-permute-start(bf16[136,16]{0,1:T(8,128)(2,1)} %select_bitcast_fusion.2), channel_id=1, source_target_pairs={{8,0},{16,8},{24,16},{9,1},{17,9},{25,17},{10,2},{18,10},{26,18},{... | collective-permute-start | bytes 13064 | tf_op jit(solution)/shard_map/ppermute | solution.py:11
  6.7 489.0 %collective-permute-start = (bf16[136,16]{0,1:T(8,128)(2,1)}, bf16[136,16]{0,1:T(8,128)(2,1)}, u32[]{:S(2)}, u32[]{:S(2)}) collective-permute-start(bf16[136,16]{0,1:T(8,128)(2,1)} %select_bitcast_fusion.3), channel_id=1, source_target_pairs={{0,8},{8,16},{16,24},{1,9},{9,17},{17,25},{2,10},{10,18},{18,26},{... | collective-permute-start | bytes 13064 | tf_op jit(solution)/shard_map/ppermute | solution.py:11
  14.5 18.2 %copy-start.1 = (bf16[136,8]{0,1:T(8,128)(2,1)}, bf16[136,8]{0,1:T(8,128)(2,1)S(1)}, u32[]{:S(2)}) copy-start(bf16[136,8]{0,1:T(8,128)(2,1)S(1)} %fusion.11) | copy-start | bytes 6532
  15.7 462.2 %collective-permute-start.3 = (bf16[136,2]{0,1:T(2,128)(2,1)}, bf16[136,2]{0,1:T(2,128)(2,1)}, u32[]{:S(2)}, u32[]{:S(2)}) collective-permute-start(bf16[136,2]{0,1:T(2,128)(2,1)} %fusion.21), channel_id=1, source_target_pairs={{8,0},{16,8},{24,16},{9,1},{17,9},{25,17},{10,2},{18,10},{26,18},{... | collective-permute-start | bytes 1640 | tf_op jit(solution)/shard_map/ppermute | solution.py:11
  18.2 459.8 %collective-permute-start.2 = (bf16[136,2]{0,1:T(2,128)(2,1)}, bf16[136,2]{0,1:T(2,128)(2,1)}, u32[]{:S(2)}, u32[]{:S(2)}) collective-permute-start(bf16[136,2]{0,1:T(2,128)(2,1)} %fusion.20), channel_id=1, source_target_pairs={{0,8},{8,16},{16,24},{1,9},{9,17},{17,25},{2,10},{10,18},{18,26},{... | collective-permute-start | bytes 1640 | tf_op jit(solution)/shard_map/ppermute | solution.py:11
  26.2 445.0 %all-to-all-start.1 = ((bf16[136,8,4]{0,2,1:T(4,128)(2,1)}), bf16[136,8,4]{0,2,1:T(4,128)(2,1)}, u32[]{:S(2)}, u32[]{:S(2)}) async-start(bf16[136,8,4]{0,2,1:T(4,128)(2,1)} %select_bitcast_fusion.1), calls=%async_computation.1 | async-start | bytes 32768 | tf_op jit(solution)/shard_map/all_to_all | solution.py:60
  34.8 152.8 %copy-start.9 = (s32[189,8]{0,1:T(8,128)S(1)}, s32[189,8]{0,1:T(8,128)}, u32[]{:S(2)}) copy-start(s32[189,8]{0,1:T(8,128)} %param.30) | copy-start | bytes 18148
  34.8 152.8 %copy-start.3 = (s32[2528]{0:T(1024)S(1)}, s32[2528]{0:T(1024)}, u32[]{:S(2)}) copy-start(s32[2528]{0:T(1024)} %constant.255) | copy-start | bytes 30340
  187.6 16.5 %copy-start.4 = (bf16[136,64]{0,1:T(8,128)(2,1)S(1)}, bf16[136,64]{0,1:T(8,128)(2,1)}, u32[]{:S(2)}) copy-start(bf16[136,64]{0,1:T(8,128)(2,1)} %param.21) | copy-start | bytes 52228
  187.6 18.3 %copy-start.8 = (s32[189,64]{0,1:T(8,128)S(1)}, s32[189,64]{0,1:T(8,128)}, u32[]{:S(2)}) copy-start(s32[189,64]{0,1:T(8,128)} %param.27) | copy-start | bytes 145156
  206.0 152.3 %copy-start.10 = (s32[189,8]{0,1:T(8,128)S(1)}, s32[189,8]{0,1:T(8,128)}, u32[]{:S(2)}) copy-start(s32[189,8]{0,1:T(8,128)} %param.31) | copy-start | bytes 18148
  358.3 16.3 %copy-start.11 = (pred[8,32]{1,0:T(8,128)(4,1)S(1)}, pred[8,32]{1,0:T(8,128)(4,1)}, u32[]{:S(2)}) copy-start(pred[8,32]{1,0:T(8,128)(4,1)} %compare_and_fusion.2) | copy-start | bytes 772
  437.7 33.1 %copy-start.7 = (pred[316,64]{1,0:T(8,128)(4,1)S(1)}, pred[316,64]{1,0:T(8,128)(4,1)}, u32[]{:S(2)}) copy-start(pred[316,64]{1,0:T(8,128)(4,1)} %compare_and_fusion.1) | copy-start | bytes 60676
  437.7 40.3 %copy-start.2 = (bf16[136,8]{0,1:T(8,128)(2,1)S(1)}, bf16[136,8]{0,1:T(8,128)(2,1)}, u32[]{:S(2)}) copy-start(bf16[136,8]{0,1:T(8,128)(2,1)} %copy-done.1) | copy-start | bytes 6532
  471.2 24.6 %all-to-all-start = ((bf16[136,8,32]{0,2,1:T(8,128)(2,1)}), bf16[136,8,32]{0,2,1:T(8,128)(2,1)S(1)}, u32[]{:S(2)}, u32[]{:S(2)}) async-start(bf16[136,8,32]{0,2,1:T(8,128)(2,1)} %select_bitcast_fusion), calls=%async_computation | async-start | bytes 262144 | tf_op jit(solution)/shard_map/all_to_all | solution.py:60
  486.5 9.3 %copy-start.5 = (bf16[136,64]{0,1:T(8,128)(2,1)S(1)}, bf16[136,64]{0,1:T(8,128)(2,1)}, u32[]{:S(2)}) copy-start(bf16[136,64]{0,1:T(8,128)(2,1)} %param.21) | copy-start | bytes 52228
  486.5 10.0 %copy-start.6 = (s32[20480]{0:T(1024)S(1)}, s32[20480]{0:T(1024)}, u32[]{:S(2)}) copy-start(s32[20480]{0:T(1024)} %pad_clamp_fusion) | copy-start | bytes 245764
where the time goes:
time: 581 us; the launch traced here: 579 us
  local copies, waits for them, and re-layouts  524 us (90%)
  starting transfers between devices  23 us (4%)
  matrix products  18.7 us (3%)
  other arithmetic  11.7 us (2%)
    gather x4, local copies, waits for them, and re-layouts, translate(): picks = jnp.take_along_axis(lists_ext, rows_table, axis=0)  168 us
    gather x4, local copies, waits for them, and re-layouts, translate(): live = jnp.take_along_axis(flags_ext, rows_table, axis=0)  168 us
    reshape x2, local copies, waits for them, and re-layouts, shards(): offset_ops = translators.reshape(-1, coeffs, coeffs)  95.3 us
    gather x4, local copies, waits for them, and re-layouts, translate(): gathered = jnp.take(buffer, picks, axis=1)  81.8 us
    dot_general x2, matrix products, translate(): jnp.einsum('tkl,ltc->kc', offset_ops, gathered, preferred_element_type=jn...  17.7 us
    all_to_all x2, starting transfers between devices, fetch(): lax.all_to_all(row_parts, 'gy', split_axis=1, concat_axis=1, tiled=True)  11.8 us
  transfers between devices with their start and end apart: 6, of which 0 were waited for; matrix products, arithmetic and copies ran while one was open for 81% of the time, Pallas kernels for 0%

commit v1 on v0

--- a/solution.py
+++ b/solution.py
@@ -1,7 +1,12 @@
+import functools
+
 import jax
 import jax.numpy as jnp
+import ml_dtypes
 import numpy as np
 from jax import lax
+from jax.experimental import pallas as pl
+from jax.experimental.pallas import tpu as pltpu
 from jax.sharding import PartitionSpec as P
 
 
@@ -35,13 +40,176 @@
     return result
 
 
-def entry_of_offset(dir_table, offset_count):
-    entries = dir_table.shape[1]
-    inverse = np.full((offset_count, 8), entries, np.int32)
+def entry_to_lane():
+    table = direction_table()
+    result = np.zeros((8, 189, 512), np.float32)
     for octant in range(8):
-        for entry in range(entries):
-            inverse[dir_table[octant, entry], octant] = entry
-    return inverse
+        for entry in range(189):
+            row, half = divmod(int(table[octant, entry]), 2)
+            if row < 128:
+                result[octant, entry, 128 * half + row] = 1
+            else:
+                for copy in range(4):
+                    result[octant, entry, 256 + 128 * half + 32 * copy + row - 128] = 1
+    return result.astype(ml_dtypes.bfloat16)
+
+
+K = 136
+LB = 17
+MAIN = LB * 128
+DEPTH = MAIN + 640
+ROWS = 158
+WIDE = 17 * 128
+BF16 = jnp.bfloat16
+F32 = jnp.float32
+
+
+def translate_kernel(src_f, src_c, lists, perm, trans, out_f, out_c, idx, v, g0, g1, r):
+    step = pl.program_id(0)
+    cells = out_f.shape[1]
+    coarse_cells = out_c.shape[1]
+
+    @pl.when(step == 0)
+    def _():
+        for o in range(8):
+            both = jnp.dot(lists[o], perm[o], preferred_element_type=F32)
+            idx[16 * o : 16 * o + 16] = (both[:16] * 64.0 + both[16:]).astype(jnp.int32) - 1
+        v[MAIN + LB * 32 :, :] = jnp.zeros((DEPTH - MAIN - LB * 32, WIDE), BF16)
+
+    first = jnp.where(step < 8, 16 * step, MAIN + 16 * (step - 8))
+    stride = jnp.where(step < 8, 128, 32)
+    lane = lax.broadcasted_iota(jnp.int32, (16, 128), 1)
+    live = (lax.broadcasted_iota(jnp.int32, (16, 128), 0) + 16 * step) < ROWS
+    bits = [(lane // (8 << b)) % 2 == 1 for b in range(4)]
+
+    def group(g, carry):
+        base = pl.multiple_of(g * WIDE, 128)
+        d = [jnp.where(live, trans[:, pl.ds(base + 128 * j, 128)], 0.0) for j in range(17)]
+        for b in range(4):
+            d = [jnp.where(bits[b], d[(m + (1 << b)) % 17], d[m]) for m in range(17)]
+        column = pl.multiple_of(g * 128, 128)
+        for lb in range(17):
+            piece = d[-lb % 17]
+            turn = (-8 * lb) % 128
+            if turn:
+                piece = pltpu.roll(piece, turn, 1)
+            row = pl.multiple_of(first + lb * stride, 16)
+            v[pl.ds(row, 16), pl.ds(column, 128)] = piece
+        return carry
+
+    lax.fori_loop(0, 17, group, 0)
+
+    quarter = lax.broadcasted_iota(jnp.int32, (16, 128), 1) // 32
+
+    def fetch_pair(src, low_row, high_row, out_row):
+        places = lax.broadcasted_iota(jnp.int32, (src.shape[1], 512), 0)
+        both = []
+        for place in (low_row, high_row):
+            hot = jnp.where(places == idx[pl.ds(place, 1), :], 1.0, 0.0).astype(BF16)
+            both.append(jnp.dot(src[...], hot, preferred_element_type=F32))
+        tiles = [
+            jnp.concatenate([x[8 * lb : 8 * lb + 8] for x in both], axis=0) for lb in range(LB)
+        ]
+        rows = pl.ds(pl.multiple_of(out_row, 16), 16)
+        for half, g in ((0, g0), (1, g1)):
+            for lb in range(LB):
+                g[rows, 128 * lb : 128 * lb + 128] = tiles[lb][:, 128 * half : 128 * half + 128].astype(BF16)
+            for m in range(5):
+                total = jnp.zeros((16, 128), F32)
+                for j in range(4):
+                    if 4 * m + j < LB:
+                        part = tiles[4 * m + j][:, 256 + 128 * half : 384 + 128 * half]
+                        total = jnp.where(quarter == j, part, total)
+                g[rows, MAIN + 128 * m : MAIN + 128 * m + 128] = total.astype(BF16)
+
+    @pl.when(step < cells // 8)
+    def _():
+        def pair(i, carry):
+            fetch_pair(src_f, 32 * i + step, 32 * i + 16 + step, 64 * step + 16 * i)
+            return carry
+
+        lax.fori_loop(0, 4, pair, 0)
+
+    @pl.when(step == 8)
+    def _():
+        def pair(i, carry):
+            fetch_pair(src_c, 32 * i + 8, 32 * i + 24, 8 * cells + 16 * i)
+            return carry
+
+        lax.fori_loop(0, coarse_cells // 2, pair, 0)
+
+    @pl.when(step == 9)
+    def _():
+        def product(g, from_column, to_column, width):
+            x = jnp.dot(g[...], v[:, pl.ds(from_column, width)], preferred_element_type=F32)
+            same = (
+                lax.broadcasted_iota(jnp.int32, x.shape, 0) % 8
+                == lax.broadcasted_iota(jnp.int32, x.shape, 1) % 8
+            )
+            x = jnp.where(same, x, 0.0).reshape(x.shape[0] // 8, 8, width).sum(axis=1)
+            r[:, pl.ds(to_column, width)] = x
+
+        def low(n, carry):
+            product(g0, pl.multiple_of(256 * n, 128), pl.multiple_of(256 * n, 128), 256)
+            return carry
+
+        def high(n, carry):
+            product(g1, pl.multiple_of(1152 + 256 * n, 128), pl.multiple_of(1280 + 256 * n, 128), 256)
+            return carry
+
+        lax.fori_loop(0, 4, low, 0)
+        lax.fori_loop(0, 4, high, 0)
+        product(g0, 1024, 1024, 128)
+        product(g1, 1024, 1152, 128)
+        column = lax.broadcasted_iota(jnp.int32, (K, 2304), 1)
+        k = jnp.where(column < 1152, column // 8, (column - 128) // 8 - K)
+        hit = jnp.where(k == lax.broadcasted_iota(jnp.int32, (K, 2304), 0), 1.0, 0.0)
+        out = lax.dot_general(
+            hit, r[...], (((1,), (1,)), ((), ())), precision=lax.Precision.HIGHEST,
+            preferred_element_type=F32,
+        )
+        out_f[...] = out[:, :cells]
+        out_c[...] = out[:, cells:]
+
+
+def translate(src_f, src_c, lists, perm, translators, cells, coarse_cells):
+    total = cells + coarse_cells
+
+    def whole(x):
+        return pl.BlockSpec(x.shape, lambda s: (0,) * x.ndim)
+
+    return pl.pallas_call(
+        translate_kernel,
+        grid=(10,),
+        in_specs=[
+            whole(src_f), whole(src_c), whole(lists), whole(perm),
+            pl.BlockSpec((16, translators.shape[1]), lambda s: (s, 0)),
+        ],
+        out_specs=[
+            pl.BlockSpec((K, cells), lambda s: (0, 0)),
+            pl.BlockSpec((K, coarse_cells), lambda s: (0, 0)),
+        ],
+        out_shape=[
+            jax.ShapeDtypeStruct((K, cells), F32),
+            jax.ShapeDtypeStruct((K, coarse_cells), F32),
+        ],
+        scratch_shapes=[
+            pltpu.VMEM((128, 512), jnp.int32),
+            pltpu.VMEM((DEPTH, WIDE), BF16),
+            pltpu.VMEM((8 * total, DEPTH), BF16),
+            pltpu.VMEM((8 * total, DEPTH), BF16),
+            pltpu.VMEM((total, 2304), F32),
+        ],
+        compiler_params=pltpu.CompilerParams(vmem_limit_bytes=56 * 2**20),
+    )(src_f, src_c, lists, perm, translators)
+
+
+def list_rows(fine_lists, fine_flags, coarse_lists, coarse_flags):
+    fine = jnp.where(fine_flags == 1, fine_lists + 1, 0).reshape(189, 8, 8)
+    coarse = jnp.where(coarse_flags == 1, coarse_lists + 1, 0).reshape(189, 1, 8)
+    both = jnp.concatenate([fine, coarse, jnp.zeros((189, 7, 8), jnp.int32)], axis=1)
+    both = jnp.transpose(both, (2, 1, 0))
+    return jnp.concatenate([both // 64, both % 64], axis=1).astype(BF16)
 
 
 def fetch(levels):
@@ -53,36 +221,22 @@
     )
     below = passed_along(upward, "gx", 1)
     above = passed_along(downward, "gx", -1)
-    row_pieces = []
     row_parts = jnp.concatenate(
         [jnp.take(level[0], level[1][0], axis=1) for level in levels], axis=2
     )
     received = lax.all_to_all(row_parts, "gy", split_axis=1, concat_axis=1, tiled=True)
+    buffers = []
+    side_start = 0
     row_start = 0
     for level in levels:
-        cap_row = level[1].shape[2]
-        row_pieces.append(received.reshape(level[0].shape[0], -1))
-        row_start = row_start + cap_row
-    buffers = []
-    side_start = 0
-    for level, from_row in zip(levels, row_pieces):
-        side_cells = level[2].shape[2]
-        buffers.append(jnp.concatenate([level[0], from_row, below, above], axis=1))
-        side_start = side_start + side_cells
+        cap = level[1].shape[2]
+        side = level[2].shape[2]
+        row = received[:, :, row_start : row_start + cap].reshape(level[0].shape[0], -1)
+        row_start += cap
+        sides = slice(side_start, side_start + side)
+        side_start += side
+        buffers.append(jnp.concatenate([level[0], row, below[:, sides], above[:, sides]], axis=1))
     return buffers
-
-
-def translate(buffer, lists, flags, offset_ops, inverse):
-    cell_count = lists.shape[1]
-    pad_row = jnp.zeros((1, cell_count), jnp.int32)
-    lists_ext = jnp.concatenate([lists, pad_row], axis=0)
-    flags_ext = jnp.concatenate([flags, pad_row], axis=0)
-    rows_table = jnp.asarray(np.tile(inverse, (1, cell_count // 8)))
-    picks = jnp.take_along_axis(lists_ext, rows_table, axis=0)
-    live = jnp.take_along_axis(flags_ext, rows_table, axis=0)
-    gathered = jnp.take(buffer, picks, axis=1)
-    gathered = jnp.where(live[None] > 0, gathered, jnp.zeros_like(gathered))
-    return jnp.einsum("tkl,ltc->kc", offset_ops, gathered, preferred_element_type=jnp.float32)
 
 
 def shards(
@@ -100,17 +254,21 @@
 ):
     coeffs = multipoles.shape[0]
     octant_ops = parent_ops.reshape(8, coeffs, coeffs)
-    offset_ops = translators.reshape(-1, coeffs, coeffs)
     children = multipoles.reshape(coeffs, -1, 8)
     coarse = jnp.einsum(
         "okl,lqo->kq", octant_ops, children, preferred_element_type=jnp.float32
     ).astype(jnp.bfloat16)
-    inverse = entry_of_offset(direction_table(), offset_ops.shape[0])
-    fine_buffer = fetch([(multipoles, fine_exports, fine_sides)])[0]
-    fine_locals = translate(fine_buffer, fine_lists, fine_flags, offset_ops, inverse)
-    coarse_buffer = fetch([(coarse, coarse_exports, coarse_sides)])[0]
-    coarse_locals = translate(coarse_buffer, coarse_lists, coarse_flags, offset_ops, inverse)
-    return (fine_locals, coarse_locals)
+    fine_buffer, coarse_buffer = fetch(
+        [(multipoles, fine_exports, fine_sides), (coarse, coarse_exports, coarse_sides)]
+    )
+    lists = list_rows(fine_lists, fine_flags, coarse_lists, coarse_flags)
+    perm = jnp.asarray(entry_to_lane())
+    return tuple(
+        translate(
+            fine_buffer, coarse_buffer, lists, perm, translators,
+            fine_lists.shape[1], coarse_lists.shape[1],
+        )
+    )
 
 
 def solution(mesh):

time: 581 us -> 88 us (0.15)
  local copies, waits for them, and re-layouts: 524 us -> 14.9 us
  Pallas kernels: 0 us -> 46.3 us
  matrix products: 18.7 us -> 1 us
  starting transfers between devices: 23 us -> 11.6 us
    gather x12 -> x0, local copies, waits for them, and re-layouts: 418 us -> none  [the longest x4 168 us: translate(): picks = jnp.take_along_axis(lists_ext, rows_table, axis=0)]
    reshape x3 -> x5, local copies, waits for them, and re-layouts: 96 us -> 0.27 us  [the longest x3 0.24 us: fetch(): received[:, :, row_start:row_start + cap].reshape(level[0].shape[0], -1)]
    pallas_call x0 -> x1, Pallas kernels: none -> 46.3 us  [translate(): pl.pallas_call(translate_kernel, grid=(10,), in_specs=[whole(src_f), whol...]
    dot_general x2 -> x0, matrix products: 17.7 us -> none  [translate(): jnp.einsum('tkl,ltc->kc', offset_ops, gathered, preferred_element_type=jn...]
    ppermute x4 -> x2, starting transfers between devices: 11.2 us -> 4.31 us  [passed_along(): return lax.ppermute(block, axis, route)]
    all_to_all x2 -> x1, starting transfers between devices: 11.8 us -> 7.25 us  [fetch(): lax.all_to_all(row_parts, 'gy', split_axis=1, concat_axis=1, tiled=True)]
  transfers between devices with their start and end apart: 6 -> 3, of which waited for: 0 -> 1; matrix products, arithmetic and copies ran while one was open for 81% -> 13% of each run, Pallas kernels for 0% -> 0%
where the time goes in v1:
time: 88 us; the launch traced here: 87.1 us
  Pallas kernels  46.3 us (53%)
  local copies, waits for them, and re-layouts  14.9 us (17%)
  starting transfers between devices  11.6 us (13%)
  other arithmetic  8.74 us (10%)
  waiting for transfers between devices  3.79 us (4%)
  matrix products  1 us (1%)
    pallas_call x1, Pallas kernels, translate(): pl.pallas_call(translate_kernel, grid=(10,), in_specs=[whole(src_f), whol...  46.3 us
    all_to_all x1, starting transfers between devices, fetch(): lax.all_to_all(row_parts, 'gy', split_axis=1, concat_axis=1, tiled=True)  7.25 us
    ppermute x2, starting transfers between devices, passed_along(): return lax.ppermute(block, axis, route)  4.31 us
    all_to_all x1, waiting for transfers between devices, fetch(): lax.all_to_all(row_parts, 'gy', split_axis=1, concat_axis=1, tiled=True)  3.79 us
    pallas_call x2, local copies, waits for them, and re-layouts, translate(): pl.pallas_call(translate_kernel, grid=(10,), in_specs=[whole(src_f), whol...  3.14 us
    reshape x1, local copies, waits for them, and re-layouts, shards(): octant_ops = parent_ops.reshape(8, coeffs, coeffs)  2.39 us
    gather x3, local copies, waits for them, and re-layouts, fetch(): jnp.take(level[0], level[1][0], axis=1)  2.37 us
    unnamed x3, local copies, waits for them, and re-layouts  1.95 us
  transfers between devices with their start and end apart: 3, of which 1 were waited for; matrix products, arithmetic and copies ran while one was open for 13% of the time, Pallas kernels for 0%

profile of v1, /device:TPU:0, one launch (start us, length us, event | category | flops | bytes accessed | tf_op | source)
XLA Modules:
  0.0 87.1 jit_solution(2840132029350142162)
XLA Ops:
  0.6 2.4 %reshape.100 = bf16[8,136,136]{2,1,0:T(8,128)(2,1)S(1)} reshape(bf16[4,36992]{1,0:T(4,128)(2,1)} %param.17) | data formatting | bytes 591872 | tf_op jit(solution)/shard_map/reshape | solution.py:256
  3.0 0.8 compare_and_fusion.3
  3.8 0.8 compare_and_fusion.4
  4.6 1.3 %gather_fusion.4 = bf16[16,136]{1,0:T(8,128)(2,1)S(1)} fusion(bf16[136,64]{0,1:T(8,128)(2,1)} %param.16, s32[1024]{0:T(1024)S(1)} %pad_clamp_fusion.1), kind=kCustom, calls=%fused_computation.2.clone | custom fusion | bytes 8768 | tf_op jit(solution)/shard_map/jit(_take)/gather | solution.py:220
  5.9 1.3 %gather_fusion.2 = bf16[16,136]{1,0:T(8,128)(2,1)S(1)} fusion(bf16[136,64]{0,1:T(8,128)(2,1)} %param.16, s32[1024]{0:T(1024)S(1)} %pad_clamp_fusion.3), kind=kCustom, calls=%fused_computation.clone | custom fusion | bytes 8768 | tf_op jit(solution)/shard_map/jit(_take)/gather | solution.py:217
  7.3 1.0 %fusion = bf16[136,8]{0,1:T(8,128)(2,1)S(1)} fusion(bf16[8,136,136]{2,1,0:T(8,128)(2,1)S(1)} %reshape.100, bf16[136,8,8]{0,2,1:T(8,128)(2,1)} %bitcast.79), kind=kOutput, calls=%fused_computation.7 | convolution fusion | flops 2368576 | bytes 315520 | tf_op jit(solution)/shard_map/okl,lqo->kq/dot_general | solution.py:258
  8.3 0.6 gather_fusion.5
  8.9 0.1 fusion.7
  8.9 0.1 select_bitcast_fusion.3
  9.0 0.1 copy.74
  9.2 1.3 %collective-permute-start.1 = (bf16[136,18]{1,0:T(8,128)(2,1)S(1)}, bf16[136,18]{1,0:T(8,128)(2,1)S(1)}, u32[]{:S(2)}, u32[]{:S(2)}) collective-permute-start(bf16[136,18]{1,0:T(8,128)(2,1)S(1)} %copy.74), channel_id=1, source_target_pairs={{8,0},{16,8},{24,16},{9,1},{17,9},{25,17},{10,2},{18,10},{26,18},{... | collective-permute-start | bytes 14696 | tf_op jit(solution)/shard_map/ppermute | solution.py:16
  10.4 0.6 gather_fusion.3
  11.0 0.1 fusion.6
  11.1 0.1 copy.73
  11.2 3.0 %collective-permute-start = (bf16[136,18]{1,0:T(8,128)(2,1)S(1)}, bf16[136,18]{1,0:T(8,128)(2,1)S(1)}, u32[]{:S(2)}, u32[]{:S(2)}) collective-permute-start(bf16[136,18]{1,0:T(8,128)(2,1)S(1)} %copy.73), channel_id=1, source_target_pairs={{0,8},{8,16},{16,24},{1,9},{9,17},{17,25},{2,10},{10,18},{18,26},{... | collective-permute-start | bytes 14696 | tf_op jit(solution)/shard_map/ppermute | solution.py:16
  14.3 0.7 compare_select_fusion.2
  14.9 0.7 compare_and_fusion.5
  15.6 0.7 compare_select_fusion
  16.3 0.7 compare_and_fusion
  17.0 0.1 copy.72
  17.1 0.1 reshape.148
  17.2 0.6 gather_fusion.1
  17.8 0.1 copy.70
  17.9 0.1 reshape.140
  18.0 1.7 %gather_fusion = bf16[256,136]{1,0:T(8,128)(2,1)S(1)} fusion(bf16[136,64]{0,1:T(8,128)(2,1)} %param.16, s32[1024]{0:T(1024)S(1)} %pad_clamp_fusion.5), kind=kCustom, calls=%fused_computation.4 | custom fusion | bytes 140288 | tf_op jit(solution)/shard_map/jit(_take)/gather | solution.py:225
  19.8 0.1 select_bitcast_fusion.2
  19.8 0.1 select_bitcast_fusion
  20.0 0.9 %reshape.169 = bf16[8,2,2448]{2,1,0:T(2,128)(2,1)} reshape(bf16[8,36,136]{2,1,0:T(8,128)(2,1)S(1)} %fusion.8) | data formatting | bytes 156672
  20.9 7.3 %all-to-all-start = ((bf16[8,2,2448]{2,1,0:T(2,128)(2,1)}), bf16[8,2,2448]{2,1,0:T(2,128)(2,1)S(1)}, u32[]{:S(2)}, u32[]{:S(2)}) async-start(bf16[8,2,2448]{2,1,0:T(2,128)(2,1)} %reshape.169), calls=%async_computation | async-start | bytes 163840 | tf_op jit(solution)/shard_map/all_to_all | solution.py:227
  28.1 0.7 add_select_fusion.2
  28.8 0.9 %select_bitcast_fusion.1 = s32[189,8,8]{0,2,1:T(8,128)S(1)} fusion(s32[189,64]{0,1:T(8,128)} %param.21, s32[189,64]{0,1:T(8,128)} %param.22), kind=kLoop, calls=%fused_computation.24 | loop fusion | flops 36288 | bytes 145152 | tf_op jit(solution)/shard_map/reshape | solution.py:208
  29.8 0.1 pad.4.clone
  29.9 0.2 fusion.1
  30.1 0.7 pad_maximum_fusion.1.lists
  30.7 0.9 copy.75
  31.6 0.1 copy.77
  31.7 0.1 slice.57
  31.8 0.0 collective-permute-done
  31.8 0.1 slice.56
  31.9 3.8 %all-to-all-done = bf16[8,2,2448]{2,1,0:T(2,128)(2,1)S(1)} async-done(((bf16[8,2,2448]{2,1,0:T(2,128)(2,1)}), bf16[8,2,2448]{2,1,0:T(2,128)(2,1)S(1)}, u32[]{:S(2)}, u32[]{:S(2)}) %all-to-all-start) | async-done | bytes 78368 | tf_op jit(solution)/shard_map/all_to_all | solution.py:227
  35.7 0.2 reshape.170
  35.9 0.1 copy.76
  36.1 0.1 copy.78
  36.2 0.8 pad_maximum_fusion.2.src_f
  37.0 0.7 pad_maximum_fusion.3.src_c
  37.7 46.3 %shard_map.131 = (f32[136,64]{1,0:T(8,128)}, f32[136,8]{1,0:T(8,128)}) custom-call(bf16[136,352]{1,0:T(8,128)(2,1)} %pad_maximum_fusion.2.src_f, bf16[136,44]{1,0:T(8,128)(2,1)} %pad_maximum_fusion.3.src_c, bf16[8,32,189]{2,1,0:T(8,128)(2,1)} %pad_maximum_fusion.1.lists, bf16[8,189,512]{2,1,0:T(8,128)(2,1)} %constant.81.clone.perm, bf16[158,36992]{1,0:T(8,128)(2,1)} %trans.1), custom_call_target="tpu_custom_call" | custom-call | tf_op jit(solution)/shard_map/pallas_call | solution.py:181
  83.9 1.6 %copy.80 = f32[136,64]{0,1:T(8,128)} copy(f32[136,64]{1,0:T(8,128)} %get-tuple-element.10) | data formatting | bytes 69632 | tf_op jit(solution)/shard_map/pallas_call | solution.py:181
  85.5 1.5 %copy.81 = f32[136,8]{0,1:T(8,128)} copy(f32[136,8]{1,0:T(8,128)} %get-tuple-element.11) | data formatting | bytes 8704 | tf_op jit(solution)/shard_map/pallas_call | solution.py:181
  (16 shorter events, 0.2 us)
Async XLA Ops:
  9.2 22.6 %collective-permute-start.1 = (bf16[136,18]{1,0:T(8,128)(2,1)S(1)}, bf16[136,18]{1,0:T(8,128)(2,1)S(1)}, u32[]{:S(2)}, u32[]{:S(2)}) collective-permute-start(bf16[136,18]{1,0:T(8,128)(2,1)S(1)} %copy.74), channel_id=1, source_target_pairs={{8,0},{16,8},{24,16},{9,1},{17,9},{25,17},{10,2},{18,10},{26,18},{... | collective-permute-start | bytes 14696 | tf_op jit(solution)/shard_map/ppermute | solution.py:16
  11.2 20.6 %collective-permute-start = (bf16[136,18]{1,0:T(8,128)(2,1)S(1)}, bf16[136,18]{1,0:T(8,128)(2,1)S(1)}, u32[]{:S(2)}, u32[]{:S(2)}) collective-permute-start(bf16[136,18]{1,0:T(8,128)(2,1)S(1)} %copy.73), channel_id=1, source_target_pairs={{0,8},{8,16},{16,24},{1,9},{9,17},{17,25},{2,10},{10,18},{18,26},{... | collective-permute-start | bytes 14696 | tf_op jit(solution)/shard_map/ppermute | solution.py:16
  20.9 14.8 %all-to-all-start = ((bf16[8,2,2448]{2,1,0:T(2,128)(2,1)}), bf16[8,2,2448]{2,1,0:T(2,128)(2,1)S(1)}, u32[]{:S(2)}, u32[]{:S(2)}) async-start(bf16[8,2,2448]{2,1,0:T(2,128)(2,1)} %reshape.169), calls=%async_computation | async-start | bytes 163840 | tf_op jit(solution)/shard_map/all_to_all | solution.py:227

commit v2 on v1

--- a/solution.py
+++ b/solution.py
@@ -8,12 +8,6 @@
 from jax.experimental import pallas as pl
 from jax.experimental.pallas import tpu as pltpu
 from jax.sharding import PartitionSpec as P
-
-
-def passed_along(block, axis, distance):
-    devices = range(lax.axis_size(axis))
-    route = [(i - distance, i) for i in devices if i - distance in devices]
-    return lax.ppermute(block, axis, route)
 
 
 def direction_table():
@@ -204,39 +198,144 @@
     )(src_f, src_c, lists, perm, translators)
 
 
-def list_rows(fine_lists, fine_flags, coarse_lists, coarse_flags):
+def round_up(count):
+    return -(-count // 16) * 16
+
+
+def list_rows(fine_lists, fine_flags, coarse_lists, coarse_flags, own, cap, peers, side):
+    row = coarse_lists - own
+    sides = row - cap * peers
+    slot = round_up(own)
+    row_slot = slot + round_up(cap) * (row // cap) + row % cap
+    side_slot = slot + round_up(cap) * peers + round_up(side) * (sides // side) + sides % side
+    coarse_places = jnp.where(row < 0, coarse_lists, jnp.where(sides < 0, row_slot, side_slot))
     fine = jnp.where(fine_flags == 1, fine_lists + 1, 0).reshape(189, 8, 8)
-    coarse = jnp.where(coarse_flags == 1, coarse_lists + 1, 0).reshape(189, 1, 8)
+    coarse = jnp.where(coarse_flags == 1, coarse_places + 1, 0).reshape(189, 1, 8)
     both = jnp.concatenate([fine, coarse, jnp.zeros((189, 7, 8), jnp.int32)], axis=1)
     both = jnp.transpose(both, (2, 1, 0))
     return jnp.concatenate([both // 64, both % 64], axis=1).astype(BF16)
 
 
-def fetch(levels):
-    upward = jnp.concatenate(
-        [jnp.take(level[0], level[2][0, 0], axis=1) for level in levels], axis=1
-    )
-    downward = jnp.concatenate(
-        [jnp.take(level[0], level[2][0, 1], axis=1) for level in levels], axis=1
-    )
-    below = passed_along(upward, "gx", 1)
-    above = passed_along(downward, "gx", -1)
-    row_parts = jnp.concatenate(
-        [jnp.take(level[0], level[1][0], axis=1) for level in levels], axis=2
-    )
-    received = lax.all_to_all(row_parts, "gy", split_axis=1, concat_axis=1, tiled=True)
-    buffers = []
-    side_start = 0
-    row_start = 0
-    for level in levels:
-        cap = level[1].shape[2]
-        side = level[2].shape[2]
-        row = received[:, :, row_start : row_start + cap].reshape(level[0].shape[0], -1)
-        row_start += cap
-        sides = slice(side_start, side_start + side)
-        side_start += side
-        buffers.append(jnp.concatenate([level[0], row, below[:, sides], above[:, sides]], axis=1))
-    return buffers
+def exchange_kernel(
+    n_gx, n_gy, plan, sel, mult, out_f, out_c, picked, buf_f, buf_c, send_sems, recv_sems
+):
+    i = lax.axis_index("gx")
+    j = lax.axis_index("gy")
+    mesh_ids = pl.DeviceIdType.MESH
+    barrier = pltpu.get_barrier_semaphore()
+    for d in range(1, n_gy):
+        peer = lax.rem(j + d, n_gy)
+        pl.semaphore_signal(barrier, inc=1, device_id=(i, peer), device_id_type=mesh_ids)
+
+    @pl.when(i > 0)
+    def _():
+        pl.semaphore_signal(barrier, inc=1, device_id=(i - 1, j), device_id_type=mesh_ids)
+
+    @pl.when(i < n_gx - 1)
+    def _():
+        pl.semaphore_signal(barrier, inc=1, device_id=(i + 1, j), device_id_type=mesh_ids)
+
+    hot = jnp.where(
+        sel[...] == lax.broadcasted_iota(jnp.int32, (sel.shape[0], mult.shape[1]), 1), 1.0, 0.0
+    ).astype(BF16)
+    values = lax.dot_general(
+        hot, mult[...], (((1,), (1,)), ((), ())), preferred_element_type=F32
+    ).astype(BF16)
+    picked[...] = values
+    pl.semaphore_wait(barrier, n_gy - 1 + jnp.where(i > 0, 1, 0) + jnp.where(i < n_gx - 1, 1, 0))
+
+    def row(start):
+        return pl.multiple_of(start, 16)
+
+    copies = []
+    for level, (buf, own, cap, side, base) in enumerate(zip((buf_f, buf_c), *plan)):
+        for d in range(1, n_gy):
+            peer = lax.rem(j + d, n_gy)
+            copy = pltpu.make_async_remote_copy(
+                src_ref=picked.at[pl.ds(row(base + own + cap * peer), cap)],
+                dst_ref=buf.at[pl.ds(row(own + cap * j), cap)],
+                send_sem=send_sems.at[level, d],
+                recv_sem=recv_sems.at[level, d],
+                device_id=(i, peer),
+                device_id_type=mesh_ids,
+            )
+            copy.start()
+            copies.append(copy)
+    neighbours = []
+    for level, (buf, own, cap, side, base) in enumerate(zip((buf_f, buf_c), *plan)):
+        first = own + cap * n_gy
+        for turn, there in ((0, i + 1), (1, i - 1)):
+            copy = pltpu.make_async_remote_copy(
+                src_ref=picked.at[pl.ds(base + first + side * turn, side)],
+                dst_ref=buf.at[pl.ds(first + side * turn, side)],
+                send_sem=send_sems.at[level, n_gy + turn],
+                recv_sem=recv_sems.at[level, n_gy + turn],
+                device_id=(there, j),
+                device_id_type=mesh_ids,
+            )
+            sends = (i < n_gx - 1) if turn == 0 else (i > 0)
+            receives = (i > 0) if turn == 0 else (i < n_gx - 1)
+            neighbours.append((copy, sends, receives))
+            pl.when(sends)(copy.start)
+
+            @pl.when(jnp.logical_not(receives))
+            def _(buf=buf, start=first + side * turn, side=side):
+                buf[pl.ds(start, side), :] = jnp.zeros((side, K), BF16)
+
+        buf[:own, :] = picked[base : base + own, :]
+        buf[pl.ds(row(own + cap * j), cap), :] = picked[pl.ds(row(base + own + cap * j), cap), :]
+    for copy in copies:
+        copy.wait_send()
+        copy.wait_recv()
+    for copy, sends, receives in neighbours:
+        pl.when(sends)(copy.wait_send)
+        pl.when(receives)(copy.wait_recv)
+    out_f[...] = buf_f[...].T
+    out_c[...] = buf_c[...].T
+
+
+def exchange(mult, coarse, fine_exports, fine_sides, coarse_exports, coarse_sides):
+    n_gx, n_gy = lax.axis_size("gx"), lax.axis_size("gy")
+    own_f, own_c = mult.shape[1], coarse.shape[1]
+
+    def rows(own, exports, sides, offset):
+        parts = [jnp.arange(own, dtype=jnp.int32)[None], exports[0], sides[0]]
+        padded = [
+            jnp.pad(p + offset, ((0, 0), (0, round_up(p.shape[1]) - p.shape[1])), constant_values=-1)
+            for p in parts
+        ]
+        return jnp.concatenate([p.reshape(-1) for p in padded])
+
+    sel_f = rows(own_f, fine_exports, fine_sides, 0)
+    sel_c = rows(own_c, coarse_exports, coarse_sides, own_f)
+    sel = jnp.concatenate([sel_f, sel_c])[:, None]
+    both = jnp.concatenate([mult, coarse], axis=1)
+    plan = (
+        (round_up(own_f), round_up(own_c)),
+        (round_up(fine_exports.shape[2]), round_up(coarse_exports.shape[2])),
+        (round_up(fine_sides.shape[2]), round_up(coarse_sides.shape[2])),
+        (0, sel_f.shape[0]),
+    )
+    vmem = pl.BlockSpec(memory_space=pltpu.VMEM)
+    return pl.pallas_call(
+        functools.partial(exchange_kernel, n_gx, n_gy, plan),
+        in_specs=[vmem, vmem],
+        out_specs=[vmem, vmem],
+        out_shape=[
+            jax.ShapeDtypeStruct((K, sel_f.shape[0]), BF16),
+            jax.ShapeDtypeStruct((K, sel_c.shape[0]), BF16),
+        ],
+        scratch_shapes=[
+            pltpu.VMEM((sel.shape[0], K), BF16),
+            pltpu.VMEM((sel_f.shape[0], K), BF16),
+            pltpu.VMEM((sel_c.shape[0], K), BF16),
+            pltpu.SemaphoreType.DMA((2, n_gy + 2)),
+            pltpu.SemaphoreType.DMA((2, n_gy + 2)),
+        ],
+        compiler_params=pltpu.CompilerParams(
+            collective_id=0, has_side_effects=True, vmem_limit_bytes=32 * 2**20
+        ),
+    )(sel, both)
 
 
 def shards(
@@ -258,10 +357,13 @@
     coarse = jnp.einsum(
         "okl,lqo->kq", octant_ops, children, preferred_element_type=jnp.float32
     ).astype(jnp.bfloat16)
-    fine_buffer, coarse_buffer = fetch(
-        [(multipoles, fine_exports, fine_sides), (coarse, coarse_exports, coarse_sides)]
-    )
-    lists = list_rows(fine_lists, fine_flags, coarse_lists, coarse_flags)
+    fine_buffer, coarse_buffer = exchange(
+        multipoles, coarse, fine_exports, fine_sides, coarse_exports, coarse_sides
+    )
+    lists = list_rows(
+        fine_lists, fine_flags, coarse_lists, coarse_flags,
+        coarse.shape[1], coarse_exports.shape[2], coarse_exports.shape[1], coarse_sides.shape[2],
+    )
     perm = jnp.asarray(entry_to_lane())
     return tuple(
         translate(

time: 88 us -> 74.5 us (0.85)
  Pallas kernels: 46.3 us -> 58.3 us
  starting transfers between devices: 11.6 us -> 0 us
  local copies, waits for them, and re-layouts: 14.9 us -> 9.92 us
  other arithmetic: 8.74 us -> 3.97 us
  waiting for transfers between devices: 3.79 us -> 0 us
    pallas_call x0 -> x1, Pallas kernels: none -> 12 us  [exchange(): pl.pallas_call(functools.partial(exchange_kernel, n_gx, n_gy, plan), in_s...]
    all_to_all x1 -> x0, starting transfers between devices: 7.25 us -> none  [fetch(): lax.all_to_all(row_parts, 'gy', split_axis=1, concat_axis=1, tiled=True)]
    gather x7 -> x0, local copies, waits for them, and re-layouts: 6.21 us -> none  [the longest x3 2.37 us: fetch(): jnp.take(level[0], level[1][0], axis=1)]
    ppermute x2 -> x0, starting transfers between devices: 4.31 us -> none  [passed_along(): return lax.ppermute(block, axis, route)]
    all_to_all x1 -> x0, waiting for transfers between devices: 3.79 us -> none  [fetch(): lax.all_to_all(row_parts, 'gy', split_axis=1, concat_axis=1, tiled=True)]
    and x4 -> x0, other arithmetic: 2.91 us -> none  [the longest x2 1.53 us: fetch(): jnp.take(level[0], level[2][0, 0], axis=1)]
    select_n x8 -> x1, other arithmetic: 2.51 us -> 0.74 us  [list_rows(): jnp.where(coarse_flags == 1, coarse_places + 1, 0).reshape(189, 1, 8)]
    reshape x4 -> x6, local copies, waits for them, and re-layouts: 0.25 us -> 1.7 us  [the longest x5 1.7 us: rows(): return jnp.concatenate([p.reshape(-1) for p in padded])]
  transfers between devices with their start and end apart: 3 -> 0, of which waited for: 1 -> 0; matrix products, arithmetic and copies ran while one was open for 13% -> 0% of each run, Pallas kernels for 0% -> 0%
where the time goes in v2:
time: 74.5 us; the launch traced here: 74 us
  Pallas kernels  58.3 us (78%)
  local copies, waits for them, and re-layouts  9.92 us (13%)
  other arithmetic  3.97 us (5%)
  matrix products  1 us (1%)
    pallas_call x1, Pallas kernels, translate(): pl.pallas_call(translate_kernel, grid=(10,), in_specs=[whole(src_f), whol...  46.3 us
    pallas_call x1, Pallas kernels, exchange(): pl.pallas_call(functools.partial(exchange_kernel, n_gx, n_gy, plan), in_s...  12 us
    pallas_call x2, local copies, waits for them, and re-layouts, translate(): pl.pallas_call(translate_kernel, grid=(10,), in_specs=[whole(src_f), whol...  3.14 us
    reshape x1, local copies, waits for them, and re-layouts, shards(): octant_ops = parent_ops.reshape(8, coeffs, coeffs)  2.4 us
    unnamed x6, local copies, waits for them, and re-layouts  2.21 us
    reshape x5, local copies, waits for them, and re-layouts, rows(): return jnp.concatenate([p.reshape(-1) for p in padded])  1.7 us

profile of v2, /device:TPU:0, one launch (start us, length us, event | category | flops | bytes accessed | tf_op | source)
XLA Modules:
  0.0 74.0 jit_solution(13655708150603554810)
XLA Ops:
  0.6 0.9 %select_bitcast_fusion = s32[189,8,8]{0,2,1:T(8,128)S(1)} fusion(s32[189,64]{0,1:T(8,128)} %param.17, s32[189,64]{0,1:T(8,128)} %param.18), kind=kLoop, calls=%fused_computation.15 | loop fusion | flops 36288 | bytes 145152 | tf_op jit(solution)/shard_map/reshape | solution.py:212
  1.5 0.7 %fusion.12 = s32[189,8]{0,1:T(8,128)S(1)} fusion(s32[189,8]{0,1:T(8,128)} %param.21, s32[189,8]{0,1:T(8,128)} %param.22), kind=kLoop, calls=%fused_computation.34 | loop fusion | flops 77112 | bytes 18144 | tf_op jit(solution)/shard_map/jit(_where)/select_n | solution.py:213
  2.3 0.1 pad.19.clone
  2.4 0.2 fusion.1
  2.6 0.7 pad_maximum_fusion.lists
  3.3 2.4 %reshape.51 = bf16[8,136,136]{2,1,0:T(8,128)(2,1)S(1)} reshape(bf16[4,36992]{1,0:T(4,128)(2,1)} %param.13) | data formatting | bytes 591872 | tf_op jit(solution)/shard_map/reshape | solution.py:355
  5.7 1.0 %fusion = bf16[136,8]{0,1:T(8,128)(2,1)S(1)} fusion(bf16[8,136,136]{2,1,0:T(8,128)(2,1)S(1)} %reshape.51, bf16[136,8,8]{0,2,1:T(8,128)(2,1)} %bitcast.36), kind=kOutput, calls=%fused_computation.1 | convolution fusion | flops 2368576 | bytes 315520 | tf_op jit(solution)/shard_map/okl,lqo->kq/dot_general | solution.py:357
  6.7 0.1 copy.31
  6.8 0.9 %copy.30 = bf16[136,64]{1,0:T(8,128)(2,1)S(1)} copy(bf16[136,64]{0,1:T(8,128)(2,1)} %param.12) | data formatting | bytes 34816 | tf_op args[0]
  7.7 0.1 pad_maximum_fusion.1.mult
  7.8 0.7 add_bitcast_fusion.1
  8.5 0.1 copy.36
  8.6 0.1 reshape.49
  8.7 0.7 add_bitcast_fusion.2
  9.4 0.1 reshape.50
  9.5 0.8 %reshape.46 = s32[256]{0:T(256)S(1)} reshape(s32[1,8,32]{2,1,0:T(8,128)} %param.15) | data formatting | bytes 2048 | tf_op jit(solution)/shard_map/reshape | solution.py:307
  10.2 0.8 %reshape.47 = s32[32]{0:T(128)S(1)} reshape(s32[1,2,16]{2,1,0:T(2,128)} %param.16) | data formatting | bytes 256 | tf_op jit(solution)/shard_map/reshape | solution.py:307
  11.0 0.1 concatenate.13
  11.1 0.1 broadcast_in_dim.17.sel
  11.2 12.0 %shard_map.131 = (bf16[136,352]{1,0:T(8,128)(2,1)S(1)}, bf16[136,176]{1,0:T(8,128)(2,1)S(1)}) custom-call(s32[528,1]{1,0:T(8,128)S(1)} %broadcast_in_dim.17.sel, bf16[136,72]{1,0:T(8,128)(2,1)S(1)} %pad_maximum_fusion.1.mult), custom_call_target="tpu_custom_call" | custom-call | tf_op jit(solution)/shard_map/pallas_call | solution.py:320
  23.2 0.0 copy-start
  23.2 0.6 copy-done
  23.8 0.0 copy-start.1
  23.8 0.6 copy-done.1
  24.5 46.3 %shard_map.132 = (f32[136,64]{1,0:T(8,128)}, f32[136,8]{1,0:T(8,128)}) custom-call(bf16[136,352]{1,0:T(8,128)(2,1)} %copy-done, bf16[136,176]{1,0:T(8,128)(2,1)} %copy-done.1, bf16[8,32,189]{2,1,0:T(8,128)(2,1)} %pad_maximum_fusion.lists, bf16[8,189,512]{2,1,0:T(8,128)(2,1)} %constant.92.clone.perm, bf16[158,36992]{1,0:T(8,128)(2,1)} %trans.1), custom_call_target="tpu_custom_call" | custom-call | tf_op jit(solution)/shard_map/pallas_call | solution.py:175
  70.8 1.6 %copy.34 = f32[136,64]{0,1:T(8,128)} copy(f32[136,64]{1,0:T(8,128)} %get-tuple-element.10) | data formatting | bytes 69632 | tf_op jit(solution)/shard_map/pallas_call | solution.py:175
  72.4 1.5 %copy.35 = f32[136,8]{0,1:T(8,128)} copy(f32[136,8]{1,0:T(8,128)} %get-tuple-element.11) | data formatting | bytes 8704 | tf_op jit(solution)/shard_map/pallas_call | solution.py:175
  (8 shorter events, 0.1 us)
Async XLA Ops:
  23.2 0.6 copy-start
  23.8 0.6 copy-start.1

commit v3 on v2

--- a/solution.py
+++ b/solution.py
@@ -58,16 +58,31 @@
 F32 = jnp.float32
 
 
-def translate_kernel(src_f, src_c, lists, perm, trans, out_f, out_c, idx, v, g0, g1, r):
+def translate_kernel(
+    jumps, src_f, src_c, fine_lists, fine_flags, coarse_lists, coarse_flags, perm, trans,
+    out_f, out_c, idx, v, g0, g1, r,
+):
     step = pl.program_id(0)
-    cells = out_f.shape[1]
-    coarse_cells = out_c.shape[1]
+    cells = out_f.shape[0]
+    coarse_cells = out_c.shape[0]
 
     @pl.when(step == 0)
     def _():
+        places = coarse_lists[...]
+        moved = places
+        for start, gap in jumps:
+            moved = moved + jnp.where(places >= start, gap, 0)
+        fine = jnp.where(fine_flags[...] == 1, fine_lists[...] + 1, 0)
+        coarse = jnp.where(coarse_flags[...] == 1, moved + 1, 0)
+        total = cells + coarse_cells
+        both = jnp.concatenate([fine, coarse], axis=0)
+        digits = jnp.concatenate([both >> 6, both & 63], axis=0).astype(F32).astype(BF16)
+        octant = lax.broadcasted_iota(jnp.int32, (total, 512), 0) % 8
+        found = jnp.zeros((total, 512), F32)
         for o in range(8):
-            both = jnp.dot(lists[o], perm[o], preferred_element_type=F32)
-            idx[16 * o : 16 * o + 16] = (both[:16] * 64.0 + both[16:]).astype(jnp.int32) - 1
+            x = jnp.dot(digits, perm[o], preferred_element_type=F32)
+            found = jnp.where(octant == o, x[:total] * 64.0 + x[total:], found)
+        idx[...] = found.astype(jnp.int32) - 1
         v[MAIN + LB * 32 :, :] = jnp.zeros((DEPTH - MAIN - LB * 32, WIDE), BF16)
 
     first = jnp.where(step < 8, 16 * step, MAIN + 16 * (step - 8))
@@ -76,30 +91,31 @@
     live = (lax.broadcasted_iota(jnp.int32, (16, 128), 0) + 16 * step) < ROWS
     bits = [(lane // (8 << b)) % 2 == 1 for b in range(4)]
 
-    def group(g, carry):
-        base = pl.multiple_of(g * WIDE, 128)
-        d = [jnp.where(live, trans[:, pl.ds(base + 128 * j, 128)], 0.0) for j in range(17)]
+    def group(g):
+        base = g * WIDE
+        d = [jnp.where(live, trans[:, base + 128 * j : base + 128 * j + 128], 0.0) for j in range(17)]
         for b in range(4):
             d = [jnp.where(bits[b], d[(m + (1 << b)) % 17], d[m]) for m in range(17)]
-        column = pl.multiple_of(g * 128, 128)
         for lb in range(17):
             piece = d[-lb % 17]
             turn = (-8 * lb) % 128
             if turn:
                 piece = pltpu.roll(piece, turn, 1)
             row = pl.multiple_of(first + lb * stride, 16)
-            v[pl.ds(row, 16), pl.ds(column, 128)] = piece
-        return carry
-
-    lax.fori_loop(0, 17, group, 0)
+            v[pl.ds(row, 16), 128 * g : 128 * g + 128] = piece
+
 
     quarter = lax.broadcasted_iota(jnp.int32, (16, 128), 1) // 32
 
     def fetch_pair(src, low_row, high_row, out_row):
-        places = lax.broadcasted_iota(jnp.int32, (src.shape[1], 512), 0)
+        places = lax.broadcasted_iota(jnp.int32, (src.shape[1], 512), 0).astype(jnp.int16)
         both = []
         for place in (low_row, high_row):
-            hot = jnp.where(places == idx[pl.ds(place, 1), :], 1.0, 0.0).astype(BF16)
+            wanted = jnp.broadcast_to(idx[pl.ds(place, 1), :], (16, 512)).astype(jnp.int16)
+            wanted = jnp.broadcast_to(wanted[None], (src.shape[1] // 16, 16, 512))
+            hot = jnp.where(
+                places == wanted.reshape(src.shape[1], 512), jnp.ones((), BF16), jnp.zeros((), BF16)
+            )
             both.append(jnp.dot(src[...], hot, preferred_element_type=F32))
         tiles = [
             jnp.concatenate([x[8 * lb : 8 * lb + 8] for x in both], axis=0) for lb in range(LB)
@@ -116,21 +132,22 @@
                         total = jnp.where(quarter == j, part, total)
                 g[rows, MAIN + 128 * m : MAIN + 128 * m + 128] = total.astype(BF16)
 
-    @pl.when(step < cells // 8)
-    def _():
-        def pair(i, carry):
-            fetch_pair(src_f, 32 * i + step, 32 * i + 16 + step, 64 * step + 16 * i)
-            return carry
-
-        lax.fori_loop(0, 4, pair, 0)
+    @pl.when(step >= 8)
+    def _():
+        for g in range(17):
+            group(g)
+
+    @pl.when(step < 8)
+    def _():
+        for g in range(17):
+            group(g)
+        for i in range(4):
+            fetch_pair(src_f, 8 * step + 2 * i, 8 * step + 2 * i + 1, 64 * step + 16 * i)
 
     @pl.when(step == 8)
     def _():
-        def pair(i, carry):
-            fetch_pair(src_c, 32 * i + 8, 32 * i + 24, 8 * cells + 16 * i)
-            return carry
-
-        lax.fori_loop(0, coarse_cells // 2, pair, 0)
+        for i in range(coarse_cells // 2):
+            fetch_pair(src_c, cells + 2 * i, cells + 2 * i + 1, 8 * cells + 16 * i)
 
     @pl.when(step == 9)
     def _():
@@ -157,63 +174,54 @@
         product(g1, 1024, 1152, 128)
         column = lax.broadcasted_iota(jnp.int32, (K, 2304), 1)
         k = jnp.where(column < 1152, column // 8, (column - 128) // 8 - K)
-        hit = jnp.where(k == lax.broadcasted_iota(jnp.int32, (K, 2304), 0), 1.0, 0.0)
-        out = lax.dot_general(
-            hit, r[...], (((1,), (1,)), ((), ())), precision=lax.Precision.HIGHEST,
-            preferred_element_type=F32,
-        )
-        out_f[...] = out[:, :cells]
-        out_c[...] = out[:, cells:]
-
-
-def translate(src_f, src_c, lists, perm, translators, cells, coarse_cells):
+        hit = jnp.where(k == lax.broadcasted_iota(jnp.int32, (K, 2304), 0), 1.0, 0.0).astype(BF16)
+        out = jnp.zeros((cells + coarse_cells, K), F32)
+        rest = r[...]
+        for _ in range(3):
+            piece = rest.astype(BF16)
+            rest = rest - piece.astype(F32)
+            out = out + lax.dot_general(
+                piece, hit, (((1,), (1,)), ((), ())), preferred_element_type=F32
+            )
+        out_f[...] = out[:cells]
+        out_c[...] = out[cells:]
+
+
+def translate(jumps, src_f, src_c, lists, perm, translators):
+    cells, coarse_cells = lists[0].shape[0], lists[2].shape[0]
     total = cells + coarse_cells
 
     def whole(x):
         return pl.BlockSpec(x.shape, lambda s: (0,) * x.ndim)
 
     return pl.pallas_call(
-        translate_kernel,
+        functools.partial(translate_kernel, jumps),
         grid=(10,),
         in_specs=[
-            whole(src_f), whole(src_c), whole(lists), whole(perm),
+            whole(src_f), whole(src_c), *[whole(x) for x in lists], whole(perm),
             pl.BlockSpec((16, translators.shape[1]), lambda s: (s, 0)),
         ],
         out_specs=[
-            pl.BlockSpec((K, cells), lambda s: (0, 0)),
-            pl.BlockSpec((K, coarse_cells), lambda s: (0, 0)),
+            pl.BlockSpec((cells, K), lambda s: (0, 0)),
+            pl.BlockSpec((coarse_cells, K), lambda s: (0, 0)),
         ],
         out_shape=[
-            jax.ShapeDtypeStruct((K, cells), F32),
-            jax.ShapeDtypeStruct((K, coarse_cells), F32),
+            jax.ShapeDtypeStruct((cells, K), F32),
+            jax.ShapeDtypeStruct((coarse_cells, K), F32),
         ],
         scratch_shapes=[
-            pltpu.VMEM((128, 512), jnp.int32),
+            pltpu.VMEM((total, 512), jnp.int32),
             pltpu.VMEM((DEPTH, WIDE), BF16),
             pltpu.VMEM((8 * total, DEPTH), BF16),
             pltpu.VMEM((8 * total, DEPTH), BF16),
             pltpu.VMEM((total, 2304), F32),
         ],
         compiler_params=pltpu.CompilerParams(vmem_limit_bytes=56 * 2**20),
-    )(src_f, src_c, lists, perm, translators)
+    )(src_f, src_c, *lists, perm, translators)
 
 
 def round_up(count):
     return -(-count // 16) * 16
-
-
-def list_rows(fine_lists, fine_flags, coarse_lists, coarse_flags, own, cap, peers, side):
-    row = coarse_lists - own
-    sides = row - cap * peers
-    slot = round_up(own)
-    row_slot = slot + round_up(cap) * (row // cap) + row % cap
-    side_slot = slot + round_up(cap) * peers + round_up(side) * (sides // side) + sides % side
-    coarse_places = jnp.where(row < 0, coarse_lists, jnp.where(sides < 0, row_slot, side_slot))
-    fine = jnp.where(fine_flags == 1, fine_lists + 1, 0).reshape(189, 8, 8)
-    coarse = jnp.where(coarse_flags == 1, coarse_places + 1, 0).reshape(189, 1, 8)
-    both = jnp.concatenate([fine, coarse, jnp.zeros((189, 7, 8), jnp.int32)], axis=1)
-    both = jnp.transpose(both, (2, 1, 0))
-    return jnp.concatenate([both // 64, both % 64], axis=1).astype(BF16)
 
 
 def exchange_kernel(
@@ -236,12 +244,9 @@
         pl.semaphore_signal(barrier, inc=1, device_id=(i + 1, j), device_id_type=mesh_ids)
 
     hot = jnp.where(
-        sel[...] == lax.broadcasted_iota(jnp.int32, (sel.shape[0], mult.shape[1]), 1), 1.0, 0.0
+        sel[...] == lax.broadcasted_iota(jnp.int32, (sel.shape[0], mult.shape[0]), 1), 1.0, 0.0
     ).astype(BF16)
-    values = lax.dot_general(
-        hot, mult[...], (((1,), (1,)), ((), ())), preferred_element_type=F32
-    ).astype(BF16)
-    picked[...] = values
+    picked[...] = jnp.dot(hot, mult[...], preferred_element_type=F32).astype(BF16)
     pl.semaphore_wait(barrier, n_gy - 1 + jnp.where(i > 0, 1, 0) + jnp.where(i < n_gx - 1, 1, 0))
 
     def row(start):
@@ -296,7 +301,7 @@
 
 def exchange(mult, coarse, fine_exports, fine_sides, coarse_exports, coarse_sides):
     n_gx, n_gy = lax.axis_size("gx"), lax.axis_size("gy")
-    own_f, own_c = mult.shape[1], coarse.shape[1]
+    own_f, own_c = mult.shape[0], coarse.shape[0]
 
     def rows(own, exports, sides, offset):
         parts = [jnp.arange(own, dtype=jnp.int32)[None], exports[0], sides[0]]
@@ -309,7 +314,7 @@
     sel_f = rows(own_f, fine_exports, fine_sides, 0)
     sel_c = rows(own_c, coarse_exports, coarse_sides, own_f)
     sel = jnp.concatenate([sel_f, sel_c])[:, None]
-    both = jnp.concatenate([mult, coarse], axis=1)
+    both = jnp.concatenate([mult, coarse], axis=0)
     plan = (
         (round_up(own_f), round_up(own_c)),
         (round_up(fine_exports.shape[2]), round_up(coarse_exports.shape[2])),
@@ -353,24 +358,23 @@
 ):
     coeffs = multipoles.shape[0]
     octant_ops = parent_ops.reshape(8, coeffs, coeffs)
-    children = multipoles.reshape(coeffs, -1, 8)
+    children = multipoles.T.reshape(-1, 8, coeffs)
     coarse = jnp.einsum(
-        "okl,lqo->kq", octant_ops, children, preferred_element_type=jnp.float32
+        "okl,qol->qk", octant_ops, children, preferred_element_type=jnp.float32
     ).astype(jnp.bfloat16)
     fine_buffer, coarse_buffer = exchange(
-        multipoles, coarse, fine_exports, fine_sides, coarse_exports, coarse_sides
+        multipoles.T, coarse, fine_exports, fine_sides, coarse_exports, coarse_sides
     )
-    lists = list_rows(
-        fine_lists, fine_flags, coarse_lists, coarse_flags,
-        coarse.shape[1], coarse_exports.shape[2], coarse_exports.shape[1], coarse_sides.shape[2],
-    )
+    own = coarse.shape[0]
+    peers, cap = coarse_exports.shape[1:]
+    side = coarse_sides.shape[2]
+    jumps = [(own, round_up(own) - own)]
+    jumps += [(own + cap * p, round_up(cap) - cap) for p in range(1, peers + 1)]
+    jumps += [(own + cap * peers + side, round_up(side) - side)]
+    lists = [x.T for x in (fine_lists, fine_flags, coarse_lists, coarse_flags)]
     perm = jnp.asarray(entry_to_lane())
-    return tuple(
-        translate(
-            fine_buffer, coarse_buffer, lists, perm, translators,
-            fine_lists.shape[1], coarse_lists.shape[1],
-        )
-    )
+    fine, coarse = translate(jumps, fine_buffer, coarse_buffer, lists, perm, translators)
+    return fine.T, coarse.T
 
 
 def solution(mesh):

time: 74.5 us -> 49.1 us (0.66)
  Pallas kernels: 58.3 us -> 39 us
  local copies, waits for them, and re-layouts: 9.92 us -> 5.66 us
  other arithmetic: 3.97 us -> 2.17 us
    pallas_call x1, Pallas kernels: 46.3 us -> 27 us  [translate(): pl.pallas_call(functools.partial(translate_kernel, jumps), grid=(10,), in...]
    pallas_call x2 -> x0, local copies, waits for them, and re-layouts: 3.14 us -> none  [translate(): pl.pallas_call(translate_kernel, grid=(10,), in_specs=[whole(src_f), whol...]
    reshape x1 -> x0, other arithmetic: 0.88 us -> none  [list_rows(): fine = jnp.where(fine_flags == 1, fine_lists + 1, 0).reshape(189, 8, 8)]
    unnamed x6 -> x5, local copies, waits for them, and re-layouts: 2.21 us -> 1.34 us
where the time goes in v3:
time: 49.1 us; the launch traced here: 48.5 us
  Pallas kernels  39 us (79%)
  local copies, waits for them, and re-layouts  5.66 us (12%)
  other arithmetic  2.17 us (4%)
  matrix products  0.99 us (2%)
  between operations  0.67 us (1%)
    pallas_call x1, Pallas kernels, translate(): pl.pallas_call(functools.partial(translate_kernel, jumps), grid=(10,), in...  27 us
    pallas_call x1, Pallas kernels, exchange(): pl.pallas_call(functools.partial(exchange_kernel, n_gx, n_gy, plan), in_s...  12 us
    reshape x1, local copies, waits for them, and re-layouts, shards(): octant_ops = parent_ops.reshape(8, coeffs, coeffs)  2.4 us
    reshape x5, local copies, waits for them, and re-layouts, rows(): return jnp.concatenate([p.reshape(-1) for p in padded])  1.7 us
    add x3, other arithmetic, rows(): p + offset  1.37 us
    unnamed x5, local copies, waits for them, and re-layouts  1.34 us
    dot_general x1, matrix products, shards(): jnp.einsum('okl,qol->qk', octant_ops, children, preferred_element_type=jn...  0.99 us

profile of v3, /device:TPU:0, one launch (start us, length us, event | category | flops | bytes accessed | tf_op | source)
XLA Modules:
  0.0 48.5 jit_solution(6857485220407330521)
XLA Ops:
  0.6 2.4 %reshape.46 = bf16[8,136,136]{2,1,0:T(8,128)(2,1)S(1)} reshape(bf16[4,36992]{1,0:T(4,128)(2,1)} %param.13) | data formatting | bytes 591872 | tf_op jit(solution)/shard_map/reshape | solution.py:360
  3.0 1.0 %fusion = bf16[8,136]{1,0:T(8,128)(2,1)S(1)} fusion(bf16[8,136,136]{2,1,0:T(8,128)(2,1)S(1)} %reshape.46, bf16[8,8,136]{2,1,0:T(8,128)(2,1)} %bitcast.20), kind=kOutput, calls=%fused_computation.1 | convolution fusion | flops 2368576 | bytes 315520 | tf_op jit(solution)/shard_map/okl,qol->qk/dot_general | solution.py:362
  4.0 0.8 %pad_maximum_fusion.mult = bf16[72,136]{1,0:T(8,128)(2,1)S(1)} fusion(bf16[8,136]{1,0:T(8,128)(2,1)S(1)} %fusion, bf16[64,136]{1,0:T(8,128)(2,1)} %bitcast.21), kind=kLoop, calls=%fused_computation.2 | loop fusion | flops 39168 | bytes 39168 | tf_op jit(solution)/shard_map/concatenate | solution.py:317
  4.8 0.7 %add_bitcast_fusion = s32[8,4]{0,1:T(4,128)S(1)} fusion(s32[1,8,4]{1,2,0:T(4,128)} %param.19), kind=kLoop, calls=%fused_computation.4 | loop fusion | flops 32 | bytes 256 | tf_op jit(solution)/shard_map/add | solution.py:309
  5.5 0.1 copy.19
  5.6 0.1 reshape.43
  5.7 0.7 %add_bitcast_fusion.1 = s32[2,2]{1,0:T(2,128)S(1)} fusion(s32[1,2,2]{2,1,0:T(2,128)} %param.20), kind=kLoop, calls=%fused_computation.5 | loop fusion | flops 4 | bytes 32 | tf_op jit(solution)/shard_map/add | solution.py:309
  6.4 0.1 reshape.44
  6.5 0.8 %reshape.40 = s32[256]{0:T(256)S(1)} reshape(s32[1,8,32]{2,1,0:T(8,128)} %param.15) | data formatting | bytes 2048 | tf_op jit(solution)/shard_map/reshape | solution.py:312
  7.2 0.8 %reshape.41 = s32[32]{0:T(128)S(1)} reshape(s32[1,2,16]{2,1,0:T(2,128)} %param.16) | data formatting | bytes 256 | tf_op jit(solution)/shard_map/reshape | solution.py:312
  8.0 0.1 concatenate.6
  8.1 0.1 broadcast_in_dim.6.sel
  8.2 12.0 %shard_map.131 = (bf16[136,352]{1,0:T(8,128)(2,1)S(1)}, bf16[136,176]{1,0:T(8,128)(2,1)S(1)}) custom-call(s32[528,1]{1,0:T(8,128)S(1)} %broadcast_in_dim.6.sel, bf16[72,136]{1,0:T(8,128)(2,1)S(1)} %pad_maximum_fusion.mult), custom_call_target="tpu_custom_call" | custom-call | tf_op jit(solution)/shard_map/pallas_call | solution.py:325
  20.2 0.0 copy-start
  20.2 0.6 %copy-done = bf16[136,352]{1,0:T(8,128)(2,1)} copy-done((bf16[136,352]{1,0:T(8,128)(2,1)}, bf16[136,352]{1,0:T(8,128)(2,1)S(1)}, u32[]{:S(2)}) %copy-start) | copy-done | bytes 95768
  20.9 0.0 copy-start.1
  20.9 0.6 %copy-done.1 = bf16[136,176]{1,0:T(8,128)(2,1)} copy-done((bf16[136,176]{1,0:T(8,128)(2,1)}, bf16[136,176]{1,0:T(8,128)(2,1)S(1)}, u32[]{:S(2)}) %copy-start.1) | copy-done | bytes 47896
  21.5 27.0 %shard_map.132 = (f32[64,136]{1,0:T(8,128)}, f32[8,136]{1,0:T(8,128)}) custom-call(bf16[136,352]{1,0:T(8,128)(2,1)} %copy-done, bf16[136,176]{1,0:T(8,128)(2,1)} %copy-done.1, s32[64,189]{1,0:T(8,128)} %bitcast.22, s32[64,189]{1,0:T(8,128)} %bitcast.23, s32[8,189]{1,0:T(8,128)} %bitcast.24, s32[8,189]{1,0:T(8,128)} %bitcast.25, ...), custom_call_target="tpu_custom_call" | custom-call | tf_op jit(solution)/shard_map/pallas_call | solution.py:197
  (5 shorter events, 0.0 us)
Async XLA Ops:
  20.2 0.6 %copy-start = (bf16[136,352]{1,0:T(8,128)(2,1)}, bf16[136,352]{1,0:T(8,128)(2,1)S(1)}, u32[]{:S(2)}) copy-start(bf16[136,352]{1,0:T(8,128)(2,1)S(1)} %get-tuple-element.6.src_f) | copy-start | bytes 287236
  20.9 0.6 %copy-start.1 = (bf16[136,176]{1,0:T(8,128)(2,1)}, bf16[136,176]{1,0:T(8,128)(2,1)S(1)}, u32[]{:S(2)}) copy-start(bf16[136,176]{1,0:T(8,128)(2,1)S(1)} %get-tuple-element.7.src_c) | copy-start | bytes 143620

commit v4 on v3

--- a/solution.py
+++ b/solution.py
@@ -91,9 +91,11 @@
     live = (lax.broadcasted_iota(jnp.int32, (16, 128), 0) + 16 * step) < ROWS
     bits = [(lane // (8 << b)) % 2 == 1 for b in range(4)]
 
-    def group(g):
+    def group(g, last=False):
         base = g * WIDE
-        d = [jnp.where(live, trans[:, base + 128 * j : base + 128 * j + 128], 0.0) for j in range(17)]
+        d = [trans[:, base + 128 * j : base + 128 * j + 128] for j in range(17)]
+        if last:
+            d = [jnp.where(live, x, 0.0) for x in d]
         for b in range(4):
             d = [jnp.where(bits[b], d[(m + (1 << b)) % 17], d[m]) for m in range(17)]
         for lb in range(17):
@@ -132,11 +134,6 @@
                         total = jnp.where(quarter == j, part, total)
                 g[rows, MAIN + 128 * m : MAIN + 128 * m + 128] = total.astype(BF16)
 
-    @pl.when(step >= 8)
-    def _():
-        for g in range(17):
-            group(g)
-
     @pl.when(step < 8)
     def _():
         for g in range(17):
@@ -146,11 +143,16 @@
 
     @pl.when(step == 8)
     def _():
+        for g in range(17):
+            group(g)
         for i in range(coarse_cells // 2):
             fetch_pair(src_c, cells + 2 * i, cells + 2 * i + 1, 8 * cells + 16 * i)
 
     @pl.when(step == 9)
     def _():
+        for g in range(17):
+            group(g, last=True)
+
         def product(g, from_column, to_column, width):
             x = jnp.dot(g[...], v[:, pl.ds(from_column, width)], preferred_element_type=F32)
             same = (
@@ -160,16 +162,9 @@
             x = jnp.where(same, x, 0.0).reshape(x.shape[0] // 8, 8, width).sum(axis=1)
             r[:, pl.ds(to_column, width)] = x
 
-        def low(n, carry):
-            product(g0, pl.multiple_of(256 * n, 128), pl.multiple_of(256 * n, 128), 256)
-            return carry
-
-        def high(n, carry):
-            product(g1, pl.multiple_of(1152 + 256 * n, 128), pl.multiple_of(1280 + 256 * n, 128), 256)
-            return carry
-
-        lax.fori_loop(0, 4, low, 0)
-        lax.fori_loop(0, 4, high, 0)
+        for n in range(4):
+            product(g0, 256 * n, 256 * n, 256)
+            product(g1, 1152 + 256 * n, 1280 + 256 * n, 256)
         product(g0, 1024, 1024, 128)
         product(g1, 1024, 1152, 128)
         column = lax.broadcasted_iota(jnp.int32, (K, 2304), 1)
@@ -225,7 +220,7 @@
 
 
 def exchange_kernel(
-    n_gx, n_gy, plan, sel, mult, out_f, out_c, picked, buf_f, buf_c, send_sems, recv_sems
+    n_gx, n_gy, plan, exp_f, side_f, sel_c, mult, out_f, out_c, picked, buf_f, buf_c, send_sems, recv_sems
 ):
     i = lax.axis_index("gx")
     j = lax.axis_index("gy")
@@ -243,10 +238,17 @@
     def _():
         pl.semaphore_signal(barrier, inc=1, device_id=(i + 1, j), device_id_type=mesh_ids)
 
+    own = plan[0][0]
+    depth = mult.shape[0]
+    wanted = [lax.broadcasted_iota(jnp.int32, (1, own), 1)]
+    wanted += [exp_f[0, p : p + 1, :] for p in range(n_gy)]
+    wanted += [side_f[0, t : t + 1, :] for t in range(2)]
+    wanted += [sel_c[p : p + 1, :] for p in range(sel_c.shape[0])]
+    wanted = jnp.concatenate(wanted, axis=1)
     hot = jnp.where(
-        sel[...] == lax.broadcasted_iota(jnp.int32, (sel.shape[0], mult.shape[0]), 1), 1.0, 0.0
-    ).astype(BF16)
-    picked[...] = jnp.dot(hot, mult[...], preferred_element_type=F32).astype(BF16)
+        wanted == lax.broadcasted_iota(jnp.int32, (depth, wanted.shape[1]), 0), 1.0, 0.0
+    )
+    picked[...] = jnp.dot(hot.T.astype(BF16), mult[...], preferred_element_type=F32).astype(BF16)
     pl.semaphore_wait(barrier, n_gy - 1 + jnp.where(i > 0, 1, 0) + jnp.where(i < n_gx - 1, 1, 0))
 
     def row(start):
@@ -303,44 +305,42 @@
     n_gx, n_gy = lax.axis_size("gx"), lax.axis_size("gy")
     own_f, own_c = mult.shape[0], coarse.shape[0]
 
-    def rows(own, exports, sides, offset):
-        parts = [jnp.arange(own, dtype=jnp.int32)[None], exports[0], sides[0]]
-        padded = [
-            jnp.pad(p + offset, ((0, 0), (0, round_up(p.shape[1]) - p.shape[1])), constant_values=-1)
+    parts = [jnp.arange(own_c, dtype=jnp.int32)[None], coarse_exports[0], coarse_sides[0]]
+    sel_c = jnp.concatenate(
+        [
+            jnp.pad(p + own_f, ((0, 0), (0, round_up(p.shape[1]) - p.shape[1])), constant_values=-1)
             for p in parts
         ]
-        return jnp.concatenate([p.reshape(-1) for p in padded])
-
-    sel_f = rows(own_f, fine_exports, fine_sides, 0)
-    sel_c = rows(own_c, coarse_exports, coarse_sides, own_f)
-    sel = jnp.concatenate([sel_f, sel_c])[:, None]
+    )
+    rows_f = own_f + fine_exports[0].size + fine_sides[0].size
+    rows_c = sel_c.size
     both = jnp.concatenate([mult, coarse], axis=0)
     plan = (
         (round_up(own_f), round_up(own_c)),
         (round_up(fine_exports.shape[2]), round_up(coarse_exports.shape[2])),
         (round_up(fine_sides.shape[2]), round_up(coarse_sides.shape[2])),
-        (0, sel_f.shape[0]),
+        (0, rows_f),
     )
     vmem = pl.BlockSpec(memory_space=pltpu.VMEM)
     return pl.pallas_call(
         functools.partial(exchange_kernel, n_gx, n_gy, plan),
-        in_specs=[vmem, vmem],
+        in_specs=[vmem] * 4,
         out_specs=[vmem, vmem],
         out_shape=[
-            jax.ShapeDtypeStruct((K, sel_f.shape[0]), BF16),
-            jax.ShapeDtypeStruct((K, sel_c.shape[0]), BF16),
+            jax.ShapeDtypeStruct((K, rows_f), BF16),
+            jax.ShapeDtypeStruct((K, rows_c), BF16),
         ],
         scratch_shapes=[
-            pltpu.VMEM((sel.shape[0], K), BF16),
-            pltpu.VMEM((sel_f.shape[0], K), BF16),
-            pltpu.VMEM((sel_c.shape[0], K), BF16),
+            pltpu.VMEM((rows_f + rows_c, K), BF16),
+            pltpu.VMEM((rows_f, K), BF16),
+            pltpu.VMEM((rows_c, K), BF16),
             pltpu.SemaphoreType.DMA((2, n_gy + 2)),
             pltpu.SemaphoreType.DMA((2, n_gy + 2)),
         ],
         compiler_params=pltpu.CompilerParams(
             collective_id=0, has_side_effects=True, vmem_limit_bytes=32 * 2**20
         ),
-    )(sel, both)
+    )(fine_exports, fine_sides, sel_c, both)
 
 
 def shards(

time: 49.1 us -> 46.3 us (0.943)
  Pallas kernels: 39 us -> 36.8 us
  local copies, waits for them, and re-layouts: 5.66 us -> 5.1 us
    pallas_call x1, Pallas kernels: 27 us -> 24.8 us  [translate(): pl.pallas_call(functools.partial(translate_kernel, jumps), grid=(10,), in...]
    reshape x5 -> x0, local copies, waits for them, and re-layouts: 1.7 us -> none  [rows(): return jnp.concatenate([p.reshape(-1) for p in padded])]
    unnamed x5 -> x8, local copies, waits for them, and re-layouts: 1.34 us -> 2.62 us
where the time goes in v4:
time: 46.3 us; the launch traced here: 45.7 us
  Pallas kernels  36.8 us (79%)
  local copies, waits for them, and re-layouts  5.1 us (11%)
  other arithmetic  2.18 us (5%)
  matrix products  0.99 us (2%)
  between operations  0.67 us (1%)
    pallas_call x1, Pallas kernels, translate(): pl.pallas_call(functools.partial(translate_kernel, jumps), grid=(10,), in...  24.8 us
    pallas_call x1, Pallas kernels, exchange(): pl.pallas_call(functools.partial(exchange_kernel, n_gx, n_gy, plan), in_s...  11.9 us
    unnamed x8, local copies, waits for them, and re-layouts  2.62 us
    reshape x1, local copies, waits for them, and re-layouts, shards(): octant_ops = parent_ops.reshape(8, coeffs, coeffs)  2.4 us
    add x3, other arithmetic, exchange(): p + own_f  1.37 us
    dot_general x1, matrix products, shards(): jnp.einsum('okl,qol->qk', octant_ops, children, preferred_element_type=jn...  0.99 us

profile of v4, /device:TPU:0, one launch (start us, length us, event | category | flops | bytes accessed | tf_op | source)
XLA Modules:
  0.0 45.7 jit_solution(13361277712677602108)
XLA Ops:
  0.6 2.4 %reshape.23 = bf16[8,136,136]{2,1,0:T(8,128)(2,1)S(1)} reshape(bf16[4,36992]{1,0:T(4,128)(2,1)} %param.13) | data formatting | bytes 591872 | tf_op jit(solution)/shard_map/reshape | solution.py:360
  3.0 1.0 %fusion = bf16[8,136]{1,0:T(8,128)(2,1)S(1)} fusion(bf16[8,136,136]{2,1,0:T(8,128)(2,1)S(1)} %reshape.23, bf16[8,8,136]{2,1,0:T(8,128)(2,1)} %bitcast.18), kind=kOutput, calls=%fused_computation.1 | convolution fusion | flops 2368576 | bytes 315520 | tf_op jit(solution)/shard_map/okl,qol->qk/dot_general | solution.py:362
  4.0 0.8 %pad_maximum_fusion.mult = bf16[72,136]{1,0:T(8,128)(2,1)S(1)} fusion(bf16[8,136]{1,0:T(8,128)(2,1)S(1)} %fusion, bf16[64,136]{1,0:T(8,128)(2,1)} %bitcast.19), kind=kLoop, calls=%fused_computation.2 | loop fusion | flops 39168 | bytes 39168 | tf_op jit(solution)/shard_map/concatenate | solution.py:317
  4.8 0.7 %add_bitcast_fusion = s32[8,4]{0,1:T(4,128)S(1)} fusion(s32[1,8,4]{1,2,0:T(4,128)} %param.19), kind=kLoop, calls=%fused_computation.11 | loop fusion | flops 32 | bytes 256 | tf_op jit(solution)/shard_map/add | solution.py:311
  5.5 0.1 copy.14
  5.6 0.7 %add_bitcast_fusion.1 = s32[2,2]{1,0:T(2,128)S(1)} fusion(s32[1,2,2]{2,1,0:T(2,128)} %param.20), kind=kLoop, calls=%fused_computation.12 | loop fusion | flops 4 | bytes 32 | tf_op jit(solution)/shard_map/add | solution.py:311
  6.3 0.0 copy-start.2
  6.3 0.7 %copy-done.2 = s32[1,8,32]{2,1,0:T(8,128)S(1)} copy-done((s32[1,8,32]{2,1,0:T(8,128)S(1)}, s32[1,8,32]{2,1,0:T(8,128)}, u32[]{:S(2)}) %copy-start.2) | copy-done | bytes 1048
  7.0 0.0 copy-start.3
  7.0 0.7 %copy-done.3 = s32[1,2,16]{2,1,0:T(2,128)S(1)} copy-done((s32[1,2,16]{2,1,0:T(2,128)S(1)}, s32[1,2,16]{2,1,0:T(2,128)}, u32[]{:S(2)}) %copy-start.3) | copy-done | bytes 152
  7.7 11.9 %shard_map.131 = (bf16[136,352]{1,0:T(8,128)(2,1)S(1)}, bf16[136,176]{1,0:T(8,128)(2,1)S(1)}) custom-call(s32[1,8,32]{2,1,0:T(8,128)S(1)} %copy-done.2, s32[1,2,16]{2,1,0:T(2,128)S(1)} %copy-done.3, s32[11,16]{1,0:T(8,128)S(1)} %select_add_fusion.sel_c, bf16[72,136]{1,0:T(8,128)(2,1)S(1)} %pad_maximum_fusion.mult), custom_call_target="tpu_custom_call" | custom-call | tf_op jit(solution)/shard_map/pallas_call | solution.py:325
  19.6 0.0 copy-start
  19.6 0.6 %copy-done = bf16[136,352]{1,0:T(8,128)(2,1)} copy-done((bf16[136,352]{1,0:T(8,128)(2,1)}, bf16[136,352]{1,0:T(8,128)(2,1)S(1)}, u32[]{:S(2)}) %copy-start) | copy-done | bytes 95768
  20.2 0.0 copy-start.1
  20.2 0.6 %copy-done.1 = bf16[136,176]{1,0:T(8,128)(2,1)} copy-done((bf16[136,176]{1,0:T(8,128)(2,1)}, bf16[136,176]{1,0:T(8,128)(2,1)S(1)}, u32[]{:S(2)}) %copy-start.1) | copy-done | bytes 47896
  20.8 24.8 %shard_map.132 = (f32[64,136]{1,0:T(8,128)}, f32[8,136]{1,0:T(8,128)}) custom-call(bf16[136,352]{1,0:T(8,128)(2,1)} %copy-done, bf16[136,176]{1,0:T(8,128)(2,1)} %copy-done.1, s32[64,189]{1,0:T(8,128)} %bitcast.20, s32[64,189]{1,0:T(8,128)} %bitcast.21, s32[8,189]{1,0:T(8,128)} %bitcast.22, s32[8,189]{1,0:T(8,128)} %bitcast.23, ...), custom_call_target="tpu_custom_call" | custom-call | tf_op jit(solution)/shard_map/pallas_call | solution.py:192
  (2 shorter events, 0.0 us)
Async XLA Ops:
  6.3 0.7 %copy-start.2 = (s32[1,8,32]{2,1,0:T(8,128)S(1)}, s32[1,8,32]{2,1,0:T(8,128)}, u32[]{:S(2)}) copy-start(s32[1,8,32]{2,1,0:T(8,128)} %exp_f.1) | copy-start | bytes 3076
  7.0 0.7 %copy-start.3 = (s32[1,2,16]{2,1,0:T(2,128)S(1)}, s32[1,2,16]{2,1,0:T(2,128)}, u32[]{:S(2)}) copy-start(s32[1,2,16]{2,1,0:T(2,128)} %side_f.1) | copy-start | bytes 388
  19.6 0.6 %copy-start = (bf16[136,352]{1,0:T(8,128)(2,1)}, bf16[136,352]{1,0:T(8,128)(2,1)S(1)}, u32[]{:S(2)}) copy-start(bf16[136,352]{1,0:T(8,128)(2,1)S(1)} %get-tuple-element.6.src_f) | copy-start | bytes 287236
  20.2 0.6 %copy-start.1 = (bf16[136,176]{1,0:T(8,128)(2,1)}, bf16[136,176]{1,0:T(8,128)(2,1)S(1)}, u32[]{:S(2)}) copy-start(bf16[136,176]{1,0:T(8,128)(2,1)S(1)} %get-tuple-element.7.src_c) | copy-start | bytes 143620
